TPU v7x, 32 devices: a whole 2x2x4 slice. The times are simulated.
32 devices in a mesh: dp: 8 (over z, core), loop: 4 (over y, x).
Axes of the slice: x: 2, y: 2, z: 4, core: 2. Of those that a mesh axis runs over, the one named last changes fastest.
Arguments:
- crop_tokens: bfloat16 [2048, 64, 1152], P(('dp', 'loop')), may hold values from -6 to 6
- crop_lengths: int32 [32, 64], P(('dp', 'loop')), may hold values from 1 to 64, 3072 in all within a row
- crop_owner: int32 [2048, 1], P(('dp', 'loop')), may hold values from 0 to 7; in each aligned block of 64 rows (0 to 63, 64 to 127, ...) at most 16 rows name the same one
- crop_slot: int32 [2048], P(('dp', 'loop')), may hold values from 0 to 31
- base_tokens: bfloat16 [1024, 32, 1152], P(('dp', 'loop')), may hold values from -1024 to 1024
- key_probe: bfloat16 [1152, 16], replicated, may hold values from -1 to 1
- value_weight: bfloat16 [1152, 1152], replicated, may hold values from -0.1875 to 0.1875
- out_weight: bfloat16 [1152, 1152], replicated, may hold values from -0.1875 to 0.1875
- text_embed: bfloat16 [1024, 1152], P(('dp', 'loop')), may hold values from -6 to 6
- pair_labels: int32 [1024], P(('dp', 'loop')), may hold values from 0 to 31
- logit_scale: float32 [1], replicated, may hold values from 2 to 8
- logit_bias: float32 [1], replicated, may hold values from -4 to -1
Outputs:
- image_embed: bfloat16 [1024, 1152], P(('dp', 'loop'))
- image_grad: float32 [1024, 1152], P(('dp', 'loop'))
- text_grad: float32 [1024, 1152], P(('dp', 'loop'))
Inputs may be any that keep to these rules, and one draw needn't show every extreme that they name: `crop_owner`: at most 16 of the crops of one device name the same owner, and in every draw the crops of some device name one owner exactly 16 times. `crop_lengths`: the lengths of one device's crops sum to 3072 and the longest is exactly 64.
All inputs are finite; a program needn't handle non-finite values.
Results may differ from a plain program's by a relative error of at most 0.01.
Values may be sent and summed in bfloat16 or wider, within the bound.
A program may use at most 192 MiB of HBM per device.

v0:
```python
import math

import jax
import jax.numpy as jnp
from jax import lax
from jax.sharding import PartitionSpec as P

very_low = -1e30
norm_eps = 1e-06
highest = lax.Precision.HIGHEST


def crop_partial(tokens, lengths, key_probe, value_weight):
    lead_shape = tokens.shape[:-2]
    crop_width = tokens.shape[-2]
    model_width = tokens.shape[-1]
    head_count = key_probe.shape[1]
    head_dim = model_width // head_count
    flat_rows = tokens.reshape(-1, model_width)
    scores = jnp.dot(flat_rows, key_probe, preferred_element_type=jnp.float32) / math.sqrt(head_dim)
    scores = scores.reshape(lead_shape + (crop_width, head_count))
    position = lax.broadcasted_iota(jnp.int32, lead_shape + (crop_width,), len(lead_shape))
    is_valid = (position < lengths[..., None])[..., None]
    masked = jnp.where(is_valid, scores, very_low)
    maxima = jnp.max(masked, axis=-2)
    weight = jnp.where(is_valid, jnp.exp(masked - maxima[..., None, :]), 0.0)
    totals = jnp.sum(weight, axis=-2)
    mixed = jnp.einsum("...kh,...kd->...hd", weight, tokens.astype(jnp.float32), precision=highest)
    value_heads = value_weight.astype(jnp.float32).reshape(model_width, head_count, head_dim)
    projected = jnp.einsum("...hd,dhe->...he", mixed, value_heads, precision=highest)
    return (projected.reshape(lead_shape + (model_width,)), maxima, totals)


def merge_parts(base_parts, arrived_parts, img_count):
    base_sum, base_max, base_total = base_parts
    mixed_sum, maxima, totals, slot_ids = arrived_parts
    slot_count, model_width = mixed_sum.shape
    head_count = maxima.shape[1]
    member = slot_ids[:, None] == lax.broadcasted_iota(jnp.int32, (1, img_count), 1)
    candidates = jnp.where(member[:, :, None], maxima[:, None, :], very_low)
    joint_max = jnp.maximum(base_max, jnp.max(candidates, axis=0))
    member_float = member.astype(jnp.float32)
    joint_at = jnp.dot(member_float, joint_max, precision=highest)
    rescale = jnp.exp(maxima - joint_at)
    base_rescale = jnp.exp(base_max - joint_max)
    scaled = (mixed_sum.reshape(slot_count, head_count, -1) * rescale[:, :, None]).reshape(
        slot_count, model_width
    )
    base_scaled = base_sum.reshape(img_count, head_count, -1) * base_rescale[:, :, None]
    collected = lax.dot_general(member_float, scaled, (((0,), (0,)), ((), ())), precision=highest)
    collected_total = lax.dot_general(
        member_float, totals * rescale, (((0,), (0,)), ((), ())), precision=highest
    )
    denominator = base_total * base_rescale + collected_total
    pooled = (base_scaled + collected.reshape(img_count, head_count, -1)) / denominator[:, :, None]
    return pooled.reshape(img_count, model_width).astype(jnp.bfloat16)


def unit_rows(matrix):
    return (matrix * lax.rsqrt(jnp.sum(matrix * matrix, axis=1, keepdims=True) + norm_eps)).astype(
        jnp.bfloat16
    )


def make_tile(image_rows, text_rows, row_labels, column_labels, scale_value, bias_value):
    logits = (
        scale_value
        * jnp.einsum("id,jd->ij", image_rows, text_rows, preferred_element_type=jnp.float32)
        + bias_value
    )
    target_sign = jnp.where(row_labels[:, None] == column_labels[None, :], 1.0, -1.0)
    return (scale_value * (-target_sign * jax.nn.sigmoid(-target_sign * logits))).astype(
        jnp.bfloat16
    )


def tile_terms(image_unit, text_block, block_labels, own_labels, scale_value, bias_value):
    grad_tile = make_tile(image_unit, text_block, own_labels, block_labels, scale_value, bias_value)
    image_term = jnp.dot(grad_tile, text_block, preferred_element_type=jnp.float32)
    text_term = jnp.einsum("ij,id->jd", grad_tile, image_unit, preferred_element_type=jnp.float32)
    return (image_term, text_term)


def per_device(
    crop_tokens,
    crop_lengths,
    crop_owner,
    crop_slot,
    base_tokens,
    key_probe,
    value_weight,
    out_weight,
    text_embed,
    pair_labels,
    logit_scale,
    logit_bias,
):
    owners = lax.axis_size("dp")
    crop_total = crop_tokens.shape[0]
    model_width = crop_tokens.shape[2]
    head_count = key_probe.shape[1]
    img_count = base_tokens.shape[0]
    capacity = max(2, (2 * crop_total + owners - 1) // owners)
    slot_count = owners * capacity
    lengths = crop_lengths.reshape(-1)
    owner_ids = crop_owner[:, 0]
    member = (owner_ids[:, None] == lax.broadcasted_iota(jnp.int32, (1, owners), 1)).astype(
        jnp.int32
    )
    running = jnp.cumsum(member, axis=0)
    send_rank = jnp.sum(member * running, axis=1) - 1
    send_index = owner_ids * capacity + send_rank
    slot_ids = (
        jnp.zeros((slot_count,), jnp.int32).at[send_index].set(crop_slot).reshape(owners, capacity)
    )
    mixed_sum, maxima, totals = crop_partial(crop_tokens, lengths, key_probe, value_weight)
    send_sum = (
        jnp.zeros((slot_count, model_width), jnp.float32)
        .at[send_index]
        .set(mixed_sum)
        .reshape(owners, capacity, model_width)
    )
    send_max = (
        jnp.full((slot_count, head_count), very_low, jnp.float32)
        .at[send_index]
        .set(maxima)
        .reshape(owners, capacity, head_count)
    )
    send_total = (
        jnp.zeros((slot_count, head_count), jnp.float32)
        .at[send_index]
        .set(totals)
        .reshape(owners, capacity, head_count)
    )
    received = (
        lax.all_to_all(send_sum, "dp", split_axis=0, concat_axis=0, tiled=True),
        lax.all_to_all(send_max, "dp", split_axis=0, concat_axis=0, tiled=True),
        lax.all_to_all(send_total, "dp", split_axis=0, concat_axis=0, tiled=True),
        lax.all_to_all(slot_ids, "dp", split_axis=0, concat_axis=0, tiled=True),
    )
    flat_parts = tuple(
        (
            received_item.reshape((slot_count,) + received_item.shape[2:])
            for received_item in received
        )
    )
    base_lengths = jnp.full((img_count,), base_tokens.shape[1], jnp.int32)
    base_parts = crop_partial(base_tokens, base_lengths, key_probe, value_weight)
    pooled = merge_parts(base_parts, flat_parts, img_count)
    features = jnp.dot(pooled, out_weight, preferred_element_type=jnp.float32)
    image_embed = features.astype(jnp.bfloat16)
    image_unit = unit_rows(features)
    text_unit = unit_rows(text_embed.astype(jnp.float32))
    scale_value = logit_scale[0]
    bias_value = logit_bias[0]
    text_block = lax.all_gather(text_unit, "loop", axis=0, tiled=True)
    block_labels = lax.all_gather(pair_labels, "loop", axis=0, tiled=True)
    image_term, text_term = tile_terms(
        image_unit, text_block, block_labels, pair_labels, scale_value, bias_value
    )
    text_grad = lax.psum_scatter(
        text_term.astype(jnp.bfloat16), "loop", scatter_dimension=0, tiled=True
    ).astype(jnp.float32)
    return (image_embed, image_term, text_grad)


def solution(mesh):
    return jax.shard_map(
        per_device,
        mesh=mesh,
        in_specs=(
            P(("dp", "loop"), None, None),
            P(("dp", "loop"), None),
            P(("dp", "loop"), None),
            P(("dp", "loop")),
            P(("dp", "loop"), None, None),
            P(),
            P(),
            P(),
            P(("dp", "loop"), None),
            P(("dp", "loop")),
            P(),
            P(),
        ),
        out_specs=(P(("dp", "loop"), None), P(("dp", "loop"), None), P(("dp", "loop"), None)),
        check_vma=False,
    )
```

profile of v0, /device:TPU:0, one launch (start us, length us, event | category | flops | bytes accessed | tf_op | source)
XLA Modules:
  0.0 163.2 jit_solution(16054795465365252032)
XLA Ops:
  11.3 6.3 %all-to-all-start = ((s32[8,1,16]{2,1,0:T(1,128)}), s32[8,1,16]{2,1,0:T(1,128)}, u32[]{:S(2)}, u32[]{:S(2)}) async-start(s32[8,1,16]{2,1,0:T(1,128)} %bitcast.6), calls=%async_computation | async-start | bytes 8192 | tf_op jit(solution)/shard_map/all_to_all | solution.py:139
  17.6 2.4 %convolution_multiply_fusion.1 = f32[1024,16]{0,1:T(8,128)S(1)} fusion(bf16[1024,1152]{1,0:T(8,128)(2,1)} %bitcast.64, bf16[1152,16]{0,1:T(8,128)(2,1)} %param.17), kind=kOutput, calls=%fused_computation.16 | convolution fusion | flops 37765120 | bytes 2461696 | tf_op jit(solution)/shard_map/dot_general | solution.py:20
  20.8 6.9 %convolution_multiply_fusion = f32[4096,16]{0,1:T(8,128)} fusion(bf16[4096,1152]{1,0:T(8,128)(2,1)} %bitcast.61, bf16[1152,16]{0,1:T(8,128)(2,1)S(1)} %copy-done.3), kind=kOutput, calls=%fused_computation.6 | convolution fusion | flops 151060480 | bytes 9736192 | tf_op jit(solution)/shard_map/dot_general | solution.py:20
  29.9 8.5 %fusion.27 = f32[64,16,1152]{2,1,0:T(8,128)} fusion(bf16[64,64,1152]{2,1,0:T(8,128)(2,1)} %param.12, f32[64,64,16]{1,0,2:T(8,128)S(1)} %reshape.135, f32[64,16]{1,0:T(8,128)S(1)} %fusion.25, pred[64,64]{1,0:T(8,128)(4,1)S(1)} %iota_compare_fusion), kind=kOutput, calls=%fused_computation.35 | convolution fusion | flops 906166272 | bytes 14426112 | tf_op jit(solution)/shard_map/...kh,...kd->...hd/dot_general | solution.py:28
  38.5 2.8 %fusion.36 = f32[32,16,1152]{2,1,0:T(8,128)} fusion(bf16[32,32,1152]{2,1,0:T(8,128)(2,1)S(1)} %copy-done.1, f32[32,32,16]{1,0,2:T(8,128)S(1)} %reshape.132, f32[32,16]{1,0:T(8,128)S(1)} %fusion.34, pred[32]{0:T(512)(128)(4,1)S(1)} %iota_compare_fusion.6), kind=kOutput, calls=%fused_computation.47 | convolution fusion | flops 226541568 | bytes 4786208 | tf_op jit(solution)/shard_map/...kh,...kd->...hd/dot_general | solution.py:28
  45.4 5.2 %copy.63 = bf16[1152,1152]{0,1:T(8,128)(2,1)} copy(bf16[1152,1152]{1,0:T(8,128)(2,1)} %param.18) | data formatting | bytes 5308416 | tf_op args[6]
  50.7 7.0 %fusion.4 = f32[64,16,72]{2,0,1:T(8,128)S(1)} fusion(bf16[1152,16,72]{0,2,1:T(8,128)(2,1)} %bitcast.62, f32[64,16,1152]{2,1,0:T(8,128)} %fusion.27), kind=kOutput, calls=%fused_computation.10 | convolution fusion | flops 1019215872 | bytes 7667712 | tf_op jit(solution)/shard_map/...hd,dhe->...he/dot_general | solution.py:30
  58.2 1.7 %scatter_custom_fusion.2 = f32[128,1152]{1,0:T(8,128)} fusion(s32[64]{0:T(128)} %copy-done.10, f32[64,1152]{1,0:T(8,128)S(1)} %reshape.161, f32[]{:T(128)} %constant.16.clone.1), kind=kCustom, calls=%fused_computation.36 | custom fusion | bytes 590336 | tf_op jit(solution)/shard_map/scatter | solution.py:120
  60.2 9.1 %all_gather.7 = bf16[128,1152]{1,0:T(8,128)(2,1)S(1)} all-gather(bf16[32,1152]{1,0:T(8,128)(2,1)S(1)} %fusion.38), channel_id=1, replica_groups=mesh['dp'=8,'loop'=4] {'loop'}, dimensions={0}, use_global_device_ids=true | all-gather | bytes 368640 | tf_op jit(solution)/shard_map/all_gather | solution.py:156
  73.3 7.9 %all-reduce = s32[128]{0:T(128)} all-reduce(s32[128]{0:T(128)S(1)} %dynamic-update-slice), channel_id=1, replica_groups=mesh['dp'=8,'loop'=4] {'loop'}, use_global_device_ids=true, to_apply=%add | all-reduce | flops 128 | bytes 1024
  81.2 5.1 %all-to-all-start.1 = ((f32[8,1,256]{2,1,0:T(1,128)}), f32[8,1,256]{2,1,0:T(1,128)S(1)}, u32[]{:S(2)}, u32[]{:S(2)}) async-start(f32[8,1,256]{2,1,0:T(1,128)} %reshape.196), calls=%async_computation.1 | async-start | bytes 16384 | tf_op jit(solution)/shard_map/all_to_all | solution.py:137
  88.2 3.7 %all-to-all-done.1 = f32[8,1,256]{2,1,0:T(1,128)S(1)} async-done(((f32[8,1,256]{2,1,0:T(1,128)}), f32[8,1,256]{2,1,0:T(1,128)S(1)}, u32[]{:S(2)}, u32[]{:S(2)}) %all-to-all-start.1) | async-done | bytes 8224 | tf_op jit(solution)/shard_map/all_to_all | solution.py:137
  91.9 3.3 %all-to-all-start.3 = ((f32[8,1,256]{2,1,0:T(1,128)}), f32[8,1,256]{2,1,0:T(1,128)S(1)}, u32[]{:S(2)}, u32[]{:S(2)}) async-start(f32[8,1,256]{2,1,0:T(1,128)} %reshape.198), calls=%async_computation.3 | async-start | bytes 16384 | tf_op jit(solution)/shard_map/all_to_all | solution.py:138
  97.6 3.2 %all-to-all-done.3 = f32[8,1,256]{2,1,0:T(1,128)S(1)} async-done(((f32[8,1,256]{2,1,0:T(1,128)}), f32[8,1,256]{2,1,0:T(1,128)S(1)}, u32[]{:S(2)}, u32[]{:S(2)}) %all-to-all-start.3) | async-done | bytes 8224 | tf_op jit(solution)/shard_map/all_to_all | solution.py:138
  101.4 3.5 %all-to-all-start.2 = ((f32[8,16,1152]{2,1,0:T(8,128)}), f32[8,16,1152]{2,1,0:T(8,128)S(1)}, u32[]{:S(2)}, u32[]{:S(2)}) async-start(f32[8,16,1152]{2,1,0:T(8,128)} %bitcast.66), calls=%async_computation.2 | async-start | bytes 1179648 | tf_op jit(solution)/shard_map/all_to_all | solution.py:136
  105.0 1.4 reduce.5
  107.1 1.5 copy.78
  108.6 1.5 reshape.140
  111.8 2.1 %copy.74 = f32[128,1152]{1,0:T(8,128)} copy(f32[128,1152]{0,1:T(8,128)} %bitcast.67) | data formatting | bytes 1179648 | tf_op jit(solution)/shard_map/mul | solution.py:46
  115.5 6.0 %fusion.10 = f32[32,16,72]{2,0,1:T(8,128)} fusion(bf16[1152,16,72]{0,2,1:T(8,128)(2,1)} %bitcast.63, f32[32,16,1152]{2,1,0:T(8,128)} %fusion.36, f32[32,16]{0,1:T(8,128)S(1)} %subtract_exponential_fusion), kind=kOutput, calls=%fused_computation.12 | convolution fusion | flops 509644800 | bytes 5163008 | tf_op jit(solution)/shard_map/...hd,dhe->...he/dot_general | solution.py:30
  121.6 1.9 %bitcast_multiply_fusion = f32[128,1152]{1,0:T(8,128)} fusion(f32[128,1152]{1,0:T(8,128)} %copy.74, f32[8,16,1152]{2,1,0:T(8,128)S(1)} %all-to-all-done.2), kind=kLoop, calls=%fused_computation.30 | loop fusion | flops 147456 | bytes 1769472 | tf_op jit(solution)/shard_map/mul | solution.py:46
  124.9 1.8 %fusion.14 = bf16[32,16,72]{2,0,1:T(8,128)(2,1)S(1)} fusion(f32[32,16,72]{2,0,1:T(8,128)} %fusion.10, f32[16,72,128]{2,1,0:T(8,128)S(1)} %bitcast.68, f32[32,16]{0,1:T(8,128)S(1)} %convolution_add_fusion.1, s32[128]{0:T(128)S(1)} %copy-done.7), kind=kOutput, calls=%fused_computation.15 | convolution fusion | flops 56737792 | bytes 813568 | tf_op jit(solution)/shard_map/dot_general | solution.py:50
  131.1 23.7 %reduce-scatter.2.cloned.1.call-done = bf16[32,1152]{1,0:T(8,128)(2,1)} async-done(((bf16[128,1152]{1,0:T(8,128)(2,1)}), bf16[32,1152]{1,0:T(8,128)(2,1)}) %reduce-scatter.2.cloned.1.call-update) | async-done | bytes 73744 | tf_op jit(solution)/shard_map/reduce_scatter | solution.py:161
  154.8 1.6 convert_element_type.44
  (80 shorter events, 28.8 us)
Async XLA Ops:
  7.2 119.7 %copy-start = (bf16[1152,1152]{1,0:T(8,128)(2,1)S(1)}, bf16[1152,1152]{1,0:T(8,128)(2,1)}, u32[]{:S(2)}) copy-start(bf16[1152,1152]{1,0:T(8,128)(2,1)} %param.19) | copy-start | bytes 7962628
  7.2 13.6 %copy-start.3 = (bf16[1152,16]{0,1:T(8,128)(2,1)S(1)}, bf16[1152,16]{0,1:T(8,128)(2,1)}, u32[]{:S(2)}) copy-start(bf16[1152,16]{0,1:T(8,128)(2,1)} %param.17) | copy-start | bytes 110596
  9.7 7.9 %copy-start.10 = (s32[64]{0:T(128)}, s32[64]{0:T(128)S(1)}, u32[]{:S(2)}) copy-start(s32[64]{0:T(128)S(1)} %fusion.54) | copy-start | bytes 772
  11.3 69.9 %all-to-all-start = ((s32[8,1,16]{2,1,0:T(1,128)}), s32[8,1,16]{2,1,0:T(1,128)}, u32[]{:S(2)}, u32[]{:S(2)}) async-start(s32[8,1,16]{2,1,0:T(1,128)} %bitcast.6), calls=%async_computation | async-start | bytes 8192 | tf_op jit(solution)/shard_map/all_to_all | solution.py:139
  20.7 8.1 %copy-start.8 = (s32[1,64]{1,0:T(1,128)S(1)}, s32[1,64]{1,0:T(1,128)}, u32[]{:S(2)}) copy-start(s32[1,64]{1,0:T(1,128)} %param.13) | copy-start | bytes 772
  29.9 8.5 %copy-start.1 = (bf16[32,32,1152]{2,1,0:T(8,128)(2,1)S(1)}, bf16[32,32,1152]{2,1,0:T(8,128)(2,1)}, u32[]{:S(2)}) copy-start(bf16[32,32,1152]{2,1,0:T(8,128)(2,1)} %param.16) | copy-start | bytes 7077892
  50.7 9.3 %copy-start.2 = (bf16[32,1152]{1,0:T(8,128)(2,1)S(1)}, bf16[32,1152]{1,0:T(8,128)(2,1)}, u32[]{:S(2)}) copy-start(bf16[32,1152]{1,0:T(8,128)(2,1)} %param.20) | copy-start | bytes 221188
  81.2 10.7 %all-to-all-start.1 = ((f32[8,1,256]{2,1,0:T(1,128)}), f32[8,1,256]{2,1,0:T(1,128)S(1)}, u32[]{:S(2)}, u32[]{:S(2)}) async-start(f32[8,1,256]{2,1,0:T(1,128)} %reshape.196), calls=%async_computation.1 | async-start | bytes 16384 | tf_op jit(solution)/shard_map/all_to_all | solution.py:137
  88.2 8.4 %copy-start.6 = (s32[128]{0:T(128)}, s32[128]{0:T(128)S(1)}, u32[]{:S(2)}) copy-start(s32[128]{0:T(128)S(1)} %eq.51) | copy-start | bytes 1540
  91.9 8.9 %all-to-all-start.3 = ((f32[8,1,256]{2,1,0:T(1,128)}), f32[8,1,256]{2,1,0:T(1,128)S(1)}, u32[]{:S(2)}, u32[]{:S(2)}) async-start(f32[8,1,256]{2,1,0:T(1,128)} %reshape.198), calls=%async_computation.3 | async-start | bytes 16384 | tf_op jit(solution)/shard_map/all_to_all | solution.py:138
  96.7 4.1 %copy-start.4 = (f32[128,16]{0,1:T(8,128)}, f32[128,16]{0,1:T(8,128)S(1)}, u32[]{:S(2)}) copy-start(f32[128,16]{0,1:T(8,128)S(1)} %broadcast_in_dim.104) | copy-start | bytes 24580
  100.8 0.6 copy-start.5
  101.4 20.2 %all-to-all-start.2 = ((f32[8,16,1152]{2,1,0:T(8,128)}), f32[8,16,1152]{2,1,0:T(8,128)S(1)}, u32[]{:S(2)}, u32[]{:S(2)}) async-start(f32[8,16,1152]{2,1,0:T(8,128)} %bitcast.66), calls=%async_computation.2 | async-start | bytes 1179648 | tf_op jit(solution)/shard_map/all_to_all | solution.py:136
  104.9 49.9 %reduce-scatter.2.cloned.1.call-start = ((), (), s32[]{:S(2)}) async-start(), calls=%async_computation.5 | async-start | bytes 368640 | tf_op jit(solution)/shard_map/reduce_scatter | solution.py:161
  121.4 3.4 %copy-start.7 = (s32[128]{0:T(128)S(1)}, s32[128]{0:T(128)}, u32[]{:S(2)}) copy-start(s32[128]{0:T(128)} %copy-done.6) | copy-start | bytes 1540
  123.5 4.7 %copy-start.9 = (s32[32]{0:T(128)S(1)}, s32[32]{0:T(128)}, u32[]{:S(2)}) copy-start(s32[32]{0:T(128)} %param.21) | copy-start | bytes 388
Sparse Core Ops, SparseCore 0:
  130.4 24.4 reduce-scatter.1
where the time goes:
time: 164 us; the launch traced here: 163 us
  matrix products  41.1 us (25%)
  waiting for transfers between devices  30.8 us (19%)
  local copies, waits for them, and re-layouts  27.6 us (17%)
  starting transfers between devices  18.3 us (11%)
  blocking collectives  17.1 us (10%)
  between operations  16.2 us (10%)
  other arithmetic  12.1 us (7%)
    reduce_scatter x1, waiting for transfers between devices, per_device(): lax.psum_scatter(text_term.astype(jnp.bfloat16), 'loop', scatter_dimensio...  23.7 us
    dot_general x2, matrix products, crop_partial(): jnp.einsum('...hd,dhe->...he', mixed, value_heads, precision=highest)  12.9 us
    dot_general x2, matrix products, crop_partial(): jnp.einsum('...kh,...kd->...hd', weight, tokens.astype(jnp.float32), prec...  11.3 us
    unnamed x29, local copies, waits for them, and re-layouts  10.2 us
    dot_general x2, matrix products, crop_partial(): jnp.dot(flat_rows, key_probe, preferred_element_type=jnp.float32)  9.31 us
    all_gather x1, blocking collectives, per_device(): text_block = lax.all_gather(text_unit, 'loop', axis=0, tiled=True)  9.13 us
    unnamed x1, blocking collectives  7.94 us
    all_to_all x1, starting transfers between devices, per_device(): lax.all_to_all(slot_ids, 'dp', split_axis=0, concat_axis=0, tiled=True)  6.33 us
  transfers between devices with their start and end apart: 5, of which 4 were waited for; matrix products, arithmetic and copies ran while one was open for 40% of the time, Pallas kernels for 0%

commit v1 on v0

v1 whole, which is shorter than its diff:
```python
import functools
import math

import jax
import jax.numpy as jnp
from jax import lax
from jax.experimental import pallas as pl
from jax.experimental.pallas import tpu as pltpu
from jax.sharding import PartitionSpec as P

very_low = -1e30
norm_eps = 1e-06
pack = 8
f32 = jnp.float32
bf16 = jnp.bfloat16
MESH = pl.DeviceIdType.MESH


def iota(shape, axis):
    return lax.broadcasted_iota(jnp.int32, shape, axis)


def dot(a, b, contract=((1,), (0,))):
    return lax.dot_general(a, b, (contract, ((), ())), preferred_element_type=f32)


def split(x, parts):
    pieces = []
    for _ in range(parts):
        piece = x.astype(bf16)
        pieces.append(piece)
        x = x - piece.astype(f32)
    return pieces


def to_row(column):
    n = column.shape[0]
    eye = iota((n, n), 0) == iota((n, n), 1)
    return jnp.sum(jnp.where(eye, column, 0.0), axis=0, keepdims=True)


def to_column(row):
    n = row.shape[1]
    eye = iota((n, n), 0) == iota((n, n), 1)
    return jnp.sum(jnp.where(eye, row, 0.0), axis=1, keepdims=True)


def unit_rows(matrix):
    total = jnp.sum(matrix * matrix, axis=1, keepdims=True)
    return (matrix * lax.rsqrt(total + norm_eps)).astype(bf16)


def step_kernel(
    dims,
    lengths_ref,
    owner_ref,
    slot_ref,
    probe_ref,
    text_ref,
    labels_ref,
    scale_ref,
    bias_ref,
    tokens_hbm,
    base_hbm,
    value_hbm,
    out_hbm,
    embed_ref,
    image_grad_ref,
    text_grad_ref,
    tokens,
    base,
    value,
    outw,
    probe_wide,
    crop_key,
    base_key,
    len_rows,
    mixed,
    peak_rows,
    total_rows,
    shares,
    base_sum,
    send,
    recv,
    text_all,
    image_all,
    load_sem,
    text_send,
    text_recv,
    crop_send,
    crop_recv,
    image_send,
    image_recv,
):
    owners, loops, cap = dims
    crops, crop_tok, width = tokens.shape
    images, base_tok, _ = base.shape
    heads = probe_ref.shape[1]
    head_dim = width // heads
    lanes = heads * pack
    crop_groups = crops // pack
    base_groups = images // pack
    wide = shares.shape[1]
    slots = owners * cap
    me = lax.axis_index("dp")
    my_loop = lax.axis_index("loop")

    barrier = pltpu.get_barrier_semaphore()
    for k in range(1, owners):
        pl.semaphore_signal(
            barrier, inc=1, device_id=(lax.rem(me + k, owners), my_loop), device_id_type=MESH
        )
    for k in range(1, loops):
        pl.semaphore_signal(
            barrier, inc=1, device_id=(me, lax.rem(my_loop + k, loops)), device_id_type=MESH
        )

    def load_crops(g):
        part = pl.ds(g * pack, pack)
        return pltpu.make_async_copy(tokens_hbm.at[part], tokens.at[part], load_sem.at[g])

    load_value = pltpu.make_async_copy(value_hbm, value, load_sem.at[crop_groups])
    load_base = pltpu.make_async_copy(base_hbm, base, load_sem.at[crop_groups + 1])
    load_out = pltpu.make_async_copy(out_hbm, outw, load_sem.at[crop_groups + 2])
    for g in range(crop_groups):
        load_crops(g).start()
    load_value.start()
    load_base.start()
    load_out.start()

    spread = (iota((heads, lanes), 1) // pack == iota((heads, lanes), 0)).astype(bf16)
    probe_wide[...] = dot(probe_ref[...], spread).astype(bf16)
    lane_of = iota((1, lanes), 1) % pack
    row = iota((pack * crop_tok, lanes), 0)
    crop_key[...] = jnp.where(row // crop_tok == lane_of, row % crop_tok, 2 * crop_tok)
    row = iota((pack * base_tok, lanes), 0)
    base_key[...] = jnp.where(row // base_tok == lane_of, 0, 2)
    lengths = lengths_ref[...].astype(f32)
    of_group = iota((crop_groups, crops), 1) // pack == iota((crop_groups, crops), 0)
    to_lane = (iota((crops, lanes), 0) % pack == iota((crops, lanes), 1) % pack).astype(bf16)
    len_rows[...] = dot(jnp.where(of_group, lengths, 0.0).astype(bf16), to_lane).astype(jnp.int32)

    text_unit = unit_rows(text_ref[...].astype(f32))
    labels = labels_ref[...].astype(f32)
    label_block = jnp.broadcast_to(to_column(labels), (images, wide - width)).astype(bf16)
    text_all[my_loop, :, :width] = text_unit
    text_all[my_loop, :, width:] = label_block

    pl.semaphore_wait(barrier, owners - 1 + loops - 1)

    def share_loop(buffer, send_sem, recv_sem):
        copies = []
        for k in range(1, loops):
            copy = pltpu.make_async_remote_copy(
                src_ref=buffer.at[my_loop],
                dst_ref=buffer.at[my_loop],
                send_sem=send_sem.at[k],
                recv_sem=recv_sem.at[k],
                device_id=(me, lax.rem(my_loop + k, loops)),
                device_id_type=MESH,
            )
            copy.start()
            copies.append(copy)
        return copies

    def await_loop(buffer, send_sem, recv_sem):
        for k in range(1, loops):
            source = lax.rem(my_loop + loops - k, loops)
            pltpu.make_async_remote_copy(
                src_ref=buffer.at[source],
                dst_ref=buffer.at[source],
                send_sem=send_sem.at[k],
                recv_sem=recv_sem.at[k],
                device_id=(me, source),
                device_id_type=MESH,
            ).wait_recv()

    text_copies = share_loop(text_all, text_send, text_recv)

    def pool_group(rows, valid, place):
        scores = dot(rows, probe_wide[...]) * (1.0 / math.sqrt(head_dim))
        masked = jnp.where(valid, scores, very_low)
        peak = jnp.max(masked, axis=0, keepdims=True)
        weight = jnp.exp(masked - peak)
        total = jnp.sum(weight, axis=0, keepdims=True)
        part = pl.ds(place, pack)
        peak_rows[part, :] = jnp.broadcast_to(peak, (pack, lanes))
        total_rows[part, :] = jnp.broadcast_to(total, (pack, lanes))
        summed = dot(weight.astype(bf16), rows, ((0,), (0,)))
        return summed.reshape(heads, pack, width)

    def crop_pair(i, carry):
        found = []
        for half in range(2):
            g = 2 * i + half
            load_crops(g).wait()
            rows = tokens[pl.ds(g * pack, pack)].reshape(pack * crop_tok, width)
            valid = crop_key[...] < len_rows[pl.ds(g, 1), :]
            found.append(pool_group(rows, valid, pl.multiple_of(g * pack, pack)))
        place = pl.ds(pl.multiple_of(i * 2 * pack, 2 * pack), 2 * pack)
        mixed[:, place, :] = jnp.concatenate(found, axis=1).astype(bf16)
        return carry

    lax.fori_loop(0, crop_groups // 2, crop_pair, 0)

    def project(first, count, store):
        for c0 in range(0, width, 256):
            w = min(256, width - c0)
            h0, h1 = c0 // head_dim, (c0 + w - 1) // head_dim + 1
            rows = mixed[h0:h1, first : first + count, :].reshape((h1 - h0) * count, width)
            block = dot(rows, value[:, c0 : c0 + w]).reshape(h1 - h0, count, w)
            head_of = (iota((1, w), 1) + c0) // head_dim
            kept = jnp.where(head_of == h0, block[0], 0.0)
            for h in range(h0 + 1, h1):
                kept = jnp.where(head_of == h, block[h - h0], kept)
            store(c0, w, kept)

    def store_crop(c0, w, block):
        shares[:, c0 : c0 + w] = block.astype(bf16)

    def store_base(c0, w, block):
        base_sum[:, c0 : c0 + w] = block

    load_value.wait()
    project(0, crops, store_crop)

    def by_crop(rows_ref, first, count):
        keep = iota((count, lanes), 0) % pack == iota((count, lanes), 1) % pack
        return jnp.where(keep, rows_ref[first : first + count, :], 0.0)

    meta_width = wide - width
    pieces = split(by_crop(peak_rows, 0, crops), 3) + split(by_crop(total_rows, 0, crops), 3)
    n_pieces = len(pieces)
    k_index = iota((n_pieces * lanes, meta_width), 0)
    gather = k_index // lanes * heads + k_index % lanes // pack == iota(
        (n_pieces * lanes, meta_width), 1
    )
    meta = dot(jnp.concatenate(pieces, axis=1), gather.astype(bf16))
    slot_column = to_column(slot_ref[...].astype(f32))
    meta_lane = iota((crops, meta_width), 1)
    meta = jnp.where(meta_lane == n_pieces * heads, slot_column + 1.0, meta)
    shares[:, width:] = meta.astype(bf16)

    owner_column = owner_ref[...].astype(f32)
    owner_row = to_row(owner_column)
    earlier = (owner_column == owner_row) & (iota((crops, crops), 0) < iota((crops, crops), 1))
    rank = jnp.sum(jnp.where(earlier, 1.0, 0.0), axis=0, keepdims=True)
    target = (owner_row * cap + rank).astype(jnp.int32)
    chosen = (iota((slots, crops), 0) == target).astype(bf16)
    send[...] = dot(chosen, shares[...]).astype(bf16).reshape(owners, cap, wide)

    crop_copies = []
    for k in range(1, owners):
        peer = lax.rem(me + k, owners)
        copy = pltpu.make_async_remote_copy(
            src_ref=send.at[peer],
            dst_ref=recv.at[me],
            send_sem=crop_send.at[k],
            recv_sem=crop_recv.at[k],
            device_id=(peer, my_loop),
            device_id_type=MESH,
        )
        copy.start()
        crop_copies.append(copy)
    recv[me] = send[me]

    load_base.wait()

    def base_pair(i, carry):
        found = []
        for half in range(2):
            g = 2 * i + half
            rows = base[pl.ds(g * pack, pack)].reshape(pack * base_tok, width)
            place = pl.multiple_of(crops + g * pack, pack)
            found.append(pool_group(rows, base_key[...] < 1, place))
        place = pl.ds(pl.multiple_of(crops + i * 2 * pack, 2 * pack), 2 * pack)
        mixed[:, place, :] = jnp.concatenate(found, axis=1).astype(bf16)
        return carry

    lax.fori_loop(0, base_groups // 2, base_pair, 0)
    project(crops, images, store_base)
    fold = (iota((lanes, heads), 0) // pack == iota((lanes, heads), 1)).astype(bf16)

    def folded(x):
        return sum(dot(piece, fold) for piece in split(x, 3))

    base_peak = folded(by_crop(peak_rows, crops, images))
    base_total = folded(by_crop(total_rows, crops, images))
    load_out.wait()
    await_loop(text_all, text_send, text_recv)

    for k in range(1, owners):
        source = lax.rem(me + owners - k, owners)
        pltpu.make_async_remote_copy(
            src_ref=send.at[source],
            dst_ref=recv.at[source],
            send_sem=crop_send.at[k],
            recv_sem=crop_recv.at[k],
            device_id=(source, my_loop),
            device_id_type=MESH,
        ).wait_recv()

    arrived = recv[...].reshape(slots, wide)
    meta = arrived[:, width:]
    m_row, m_col = iota((meta_width, meta_width), 0), iota((meta_width, meta_width), 1)
    is_peak = (m_row < 3 * heads) & (m_row % heads == m_col)
    is_total = (m_row >= 3 * heads) & (m_row < 6 * heads) & (m_row % heads + heads == m_col)
    is_slot = (m_row == 6 * heads) & (m_col == 2 * heads)
    unpack = (is_peak | is_total | is_slot).astype(bf16)
    unpacked = dot(meta, unpack)
    crop_peak = unpacked[:, :heads]
    crop_total = unpacked[:, heads : 2 * heads]
    slot_at = unpacked[:, 2 * heads : 2 * heads + 1]
    across = dot(unpack, meta, ((0,), (1,)))
    slot_row = across[2 * heads : 2 * heads + 1, :]
    member = slot_at == iota((slots, images), 1).astype(f32) + 1.0
    member_t = slot_row == iota((images, slots), 0).astype(f32) + 1.0
    joint = base_peak
    for h in range(heads):
        best = jnp.max(jnp.where(member_t, across[h : h + 1, :], very_low), axis=1, keepdims=True)
        joint = jnp.where(iota((images, heads), 1) == h, jnp.maximum(joint, best), joint)
    member_b = jnp.where(member, 1.0, 0.0).astype(bf16)
    member_tb = jnp.where(member_t, 1.0, 0.0).astype(bf16)
    joint_at = sum(dot(member_b, piece) for piece in split(joint, 3))
    taken = slot_at > 0.5
    rescale = jnp.exp(jnp.where(taken, crop_peak - joint_at, very_low))
    base_rescale = jnp.exp(base_peak - joint)
    collected = sum(dot(member_tb, piece) for piece in split(crop_total * rescale, 3))
    inverse = 1.0 / (base_total * base_rescale + collected)
    inverse_at = sum(dot(member_b, piece) for piece in split(inverse, 2))
    widen = (iota((heads, width), 1) // head_dim == iota((heads, width), 0)).astype(bf16)
    crop_factor = sum(dot(piece, widen) for piece in split(rescale * inverse_at, 2))
    base_factor = sum(dot(piece, widen) for piece in split(base_rescale * inverse, 2))
    scaled = arrived[:, :width].astype(f32) * crop_factor
    merged = sum(dot(member_tb, piece) for piece in split(scaled, 2))
    pooled = (base_sum[...] * base_factor + merged).astype(bf16)
    features = dot(pooled, outw[...])
    embed_ref[...] = features.astype(bf16)
    image_all[my_loop] = unit_rows(features)
    image_copies = share_loop(image_all, image_send, image_recv)

    scale = scale_ref[0]
    bias = bias_ref[0]
    group = loops * images
    texts = text_all[...].reshape(group, wide)
    group_labels = texts[:, width : width + 1].astype(f32)
    sign = jnp.where(group_labels == labels, 1.0, -1.0)
    texts = texts[:, :width]

    def gradient(others, own):
        logits = scale * dot(others, own, ((1,), (1,))) + bias
        tile = (scale * (-sign / (1.0 + jnp.exp(sign * logits)))).astype(bf16)
        return dot(tile, others, ((0,), (0,)))

    image_grad_ref[...] = gradient(texts, image_all[my_loop])
    await_loop(image_all, image_send, image_recv)
    text_grad_ref[...] = gradient(
        image_all[...].reshape(group, width), text_all[my_loop, :, :width]
    )
    for copy in text_copies + crop_copies + image_copies:
        copy.wait_send()


def per_device(
    crop_tokens,
    crop_lengths,
    crop_owner,
    crop_slot,
    base_tokens,
    key_probe,
    value_weight,
    out_weight,
    text_embed,
    pair_labels,
    logit_scale,
    logit_bias,
):
    owners = lax.axis_size("dp")
    loops = lax.axis_size("loop")
    crops, crop_tok, width = crop_tokens.shape
    images, base_tok, _ = base_tokens.shape
    heads = key_probe.shape[1]
    lanes = heads * pack
    cap = max(2, (2 * crops + owners - 1) // owners)
    cap = -(-cap // 16) * 16
    wide = width + 128
    groups = crops // pack
    vmem = pl.BlockSpec(memory_space=pltpu.VMEM)
    smem = pl.BlockSpec(memory_space=pltpu.SMEM)
    hbm = pl.BlockSpec(memory_space=pl.ANY)
    flops = 2 * (crops * crop_tok + images * base_tok) * width * heads * 2
    flops += 2 * (crops + 2 * images) * width * width
    return pl.pallas_call(
        functools.partial(step_kernel, (owners, loops, cap)),
        out_shape=(
            jax.ShapeDtypeStruct((images, width), bf16),
            jax.ShapeDtypeStruct((images, width), f32),
            jax.ShapeDtypeStruct((images, width), f32),
        ),
        in_specs=[vmem] * 6 + [smem] * 2 + [hbm] * 4,
        out_specs=(vmem, vmem, vmem),
        scratch_shapes=[
            pltpu.VMEM(crop_tokens.shape, bf16),
            pltpu.VMEM(base_tokens.shape, bf16),
            pltpu.VMEM((width, width), bf16),
            pltpu.VMEM((width, width), bf16),
            pltpu.VMEM((width, lanes), bf16),
            pltpu.VMEM((pack * crop_tok, lanes), jnp.int32),
            pltpu.VMEM((pack * base_tok, lanes), jnp.int32),
            pltpu.VMEM((groups, lanes), jnp.int32),
            pltpu.VMEM((heads, crops + images, width), bf16),
            pltpu.VMEM((crops + images, lanes), f32),
            pltpu.VMEM((crops + images, lanes), f32),
            pltpu.VMEM((crops, wide), bf16),
            pltpu.VMEM((images, width), f32),
            pltpu.VMEM((owners, cap, wide), bf16),
            pltpu.VMEM((owners, cap, wide), bf16),
            pltpu.VMEM((loops, images, wide), bf16),
            pltpu.VMEM((loops, images, width), bf16),
            pltpu.SemaphoreType.DMA((groups + 3,)),
            pltpu.SemaphoreType.DMA((loops,)),
            pltpu.SemaphoreType.DMA((loops,)),
            pltpu.SemaphoreType.DMA((owners,)),
            pltpu.SemaphoreType.DMA((owners,)),
            pltpu.SemaphoreType.DMA((loops,)),
            pltpu.SemaphoreType.DMA((loops,)),
        ],
        compiler_params=pltpu.CompilerParams(
            collective_id=0, has_side_effects=True, vmem_limit_bytes=56 * 1024 * 1024
        ),
        cost_estimate=pl.CostEstimate(
            flops=flops, bytes_accessed=17 * 1024 * 1024, transcendentals=0
        ),
        name="contrastive_step",
    )(
        crop_lengths,
        crop_owner,
        crop_slot.reshape(1, crops),
        key_probe,
        text_embed,
        pair_labels.reshape(1, images),
        logit_scale,
        logit_bias,
        crop_tokens,
        base_tokens,
        value_weight,
        out_weight,
    )


def solution(mesh):
    return jax.shard_map(
        per_device,
        mesh=mesh,
        in_specs=(
            P(("dp", "loop"), None, None),
            P(("dp", "loop"), None),
            P(("dp", "loop"), None),
            P(("dp", "loop")),
            P(("dp", "loop"), None, None),
            P(),
            P(),
            P(),
            P(("dp", "loop"), None),
            P(("dp", "loop")),
            P(),
            P(),
        ),
        out_specs=(P(("dp", "loop"), None), P(("dp", "loop"), None), P(("dp", "loop"), None)),
        check_vma=False,
    )
```

time: 164 us -> 43.1 us (0.26)
  matrix products: 41.1 us -> 0 us
  Pallas kernels: 0 us -> 33.2 us
  waiting for transfers between devices: 30.8 us -> 0 us
  local copies, waits for them, and re-layouts: 27.6 us -> 7.69 us
  starting transfers between devices: 18.3 us -> 0 us
  blocking collectives: 17.1 us -> 0 us
  between operations: 16.2 us -> 1.93 us
  other arithmetic: 12.1 us -> 0 us
    dot_general x13 -> x0, matrix products: 41.1 us -> none  [the longest x2 12.9 us: crop_partial(): jnp.einsum('...hd,dhe->...he', mixed, value_heads, precision=highest)]
    pallas_call x0 -> x1, Pallas kernels: none -> 33.2 us  [per_device(): pl.pallas_call(functools.partial(step_kernel, (owners, loops, cap)), out_...]
    reduce_scatter x1 -> x0, waiting for transfers between devices: 23.7 us -> none  [per_device(): lax.psum_scatter(text_term.astype(jnp.bfloat16), 'loop', scatter_dimensio...]
    all_to_all x4 -> x0, starting transfers between devices: 18.3 us -> none  [the longest x1 6.33 us: per_device(): lax.all_to_all(slot_ids, 'dp', split_axis=0, concat_axis=0, tiled=True)]
    all_gather x1 -> x0, blocking collectives: 9.13 us -> none  [per_device(): text_block = lax.all_gather(text_unit, 'loop', axis=0, tiled=True)]
    unnamed x1 -> x0, blocking collectives: 7.94 us -> none
    all_to_all x4 -> x0, waiting for transfers between devices: 7.05 us -> none  [the longest x1 3.66 us: per_device(): lax.all_to_all(send_max, 'dp', split_axis=0, concat_axis=0, tiled=True)]
    scatter x4 -> x0, local copies, waits for them, and re-layouts: 4.56 us -> none  [the longest x1 1.72 us: per_device(): send_sum = jnp.zeros((slot_count, model_width), jnp.float32).at[send_inde...]
  transfers between devices with their start and end apart: 5 -> 0, of which waited for: 4 -> 0; matrix products, arithmetic and copies ran while one was open for 40% -> 0% of each run, Pallas kernels for 0% -> 0%
where the time goes in v1:
time: 43.1 us; the launch traced here: 42.8 us
  Pallas kernels  33.2 us (77%)
  local copies, waits for them, and re-layouts  7.69 us (18%)
  between operations  1.93 us (4%)
    pallas_call x1, Pallas kernels, per_device(): pl.pallas_call(functools.partial(step_kernel, (owners, loops, cap)), out_...  33.2 us
    unnamed x5, local copies, waits for them, and re-layouts  7.69 us

profile of v1, /device:TPU:0, one launch (start us, length us, event | category | flops | bytes accessed | tf_op | source)
XLA Modules:
  0.0 42.8 jit_solution(13341706331555315165)
XLA Ops:
  1.9 1.4 %copy.15.owner_ref = s32[64,1]{1,0:T(8,128)} copy(s32[64,1]{0,1:T(1,128)} %param.14) | data formatting | bytes 512 | tf_op args[2]
  3.3 1.6 %copy.16.probe_ref = bf16[1152,16]{1,0:T(8,128)(2,1)} copy(bf16[1152,16]{0,1:T(8,128)(2,1)} %param.17) | data formatting | bytes 73728 | tf_op args[5]
  4.9 33.2 %contrastive_step.1 = (bf16[32,1152]{1,0:T(8,128)(2,1)}, f32[32,1152]{1,0:T(8,128)}, f32[32,1152]{1,0:T(8,128)}) custom-call(s32[1,64]{1,0:T(1,128)} %lengths_ref.1, s32[64,1]{1,0:T(8,128)} %copy.15.owner_ref, s32[1,64]{1,0:T(1,128)} %bitcast.2, bf16[1152,16]{1,0:T(8,128)(2,1)} %copy.16.probe_ref, bf16[32,1152]{1,0:T(8,128)(2,1)} %text_ref.1, ...), custom_call_target="tpu_custom_call" | custom-call | flops 717225984 | bytes 17825792 | tf_op jit(solution)/shard_map/contrastive_step/pallas_call | solution.py:393
  38.1 1.5 %copy.22 = bf16[32,1152]{1,0:T(8,128)(2,1)} copy(bf16[32,1152]{1,0:T(8,128)(2,1)} %get-tuple-element.6) | data formatting | bytes 147456
  39.6 1.6 %copy.23 = f32[32,1152]{1,0:T(8,128)} copy(f32[32,1152]{1,0:T(8,128)} %get-tuple-element.7) | data formatting | bytes 294912
  41.2 1.6 %copy.24 = f32[32,1152]{1,0:T(8,128)} copy(f32[32,1152]{1,0:T(8,128)} %get-tuple-element.8) | data formatting | bytes 294912

commit v2 on v1

--- a/solution.py
+++ b/solution.py
@@ -50,14 +50,20 @@
     return (matrix * lax.rsqrt(total + norm_eps)).astype(bf16)
 
 
+def column_chunks(width):
+    first = min(256, width)
+    middle = max(first, (2 * width // 3) // 256 * 256)
+    return [(0, first), (first, middle), (middle, width)]
+
+
 def step_kernel(
     dims,
-    lengths_ref,
-    owner_ref,
-    slot_ref,
-    probe_ref,
-    text_ref,
-    labels_ref,
+    lengths_hbm,
+    owner_hbm,
+    slot_hbm,
+    probe_hbm,
+    text_hbm,
+    labels_hbm,
     scale_ref,
     bias_ref,
     tokens_hbm,
@@ -67,6 +73,12 @@
     embed_ref,
     image_grad_ref,
     text_grad_ref,
+    lengths_ref,
+    owner_ref,
+    slot_ref,
+    probe_ref,
+    text_ref,
+    labels_ref,
     tokens,
     base,
     value,
@@ -80,11 +92,20 @@
     total_rows,
     shares,
     base_sum,
-    send,
-    recv,
+    crop_factor,
+    base_factor,
+    meta_send,
+    meta_recv,
+    send_0,
+    send_1,
+    send_2,
+    recv_0,
+    recv_1,
+    recv_2,
     text_all,
     image_all,
     load_sem,
+    small_sem,
     text_send,
     text_recv,
     crop_send,
@@ -95,15 +116,29 @@
     owners, loops, cap = dims
     crops, crop_tok, width = tokens.shape
     images, base_tok, _ = base.shape
-    heads = probe_ref.shape[1]
+    heads = probe_ref.shape[0]
     head_dim = width // heads
     lanes = heads * pack
     crop_groups = crops // pack
     base_groups = images // pack
-    wide = shares.shape[1]
+    wide = text_all.shape[2]
     slots = owners * cap
     me = lax.axis_index("dp")
     my_loop = lax.axis_index("loop")
+
+    smalls = [
+        pltpu.make_async_copy(source, held, small_sem.at[i])
+        for i, (source, held) in enumerate(
+            [
+                (probe_hbm, probe_ref),
+                (lengths_hbm, lengths_ref),
+                (text_hbm, text_ref),
+                (labels_hbm, labels_ref),
+                (owner_hbm, owner_ref),
+                (slot_hbm, slot_ref),
+            ]
+        )
+    ]
 
     barrier = pltpu.get_barrier_semaphore()
     for k in range(1, owners):
@@ -122,19 +157,25 @@
     load_value = pltpu.make_async_copy(value_hbm, value, load_sem.at[crop_groups])
     load_base = pltpu.make_async_copy(base_hbm, base, load_sem.at[crop_groups + 1])
     load_out = pltpu.make_async_copy(out_hbm, outw, load_sem.at[crop_groups + 2])
+    for copy in smalls[:4]:
+        copy.start()
     for g in range(crop_groups):
         load_crops(g).start()
+    for copy in smalls[4:]:
+        copy.start()
     load_value.start()
     load_base.start()
     load_out.start()
 
     spread = (iota((heads, lanes), 1) // pack == iota((heads, lanes), 0)).astype(bf16)
-    probe_wide[...] = dot(probe_ref[...], spread).astype(bf16)
     lane_of = iota((1, lanes), 1) % pack
     row = iota((pack * crop_tok, lanes), 0)
     crop_key[...] = jnp.where(row // crop_tok == lane_of, row % crop_tok, 2 * crop_tok)
     row = iota((pack * base_tok, lanes), 0)
     base_key[...] = jnp.where(row // base_tok == lane_of, 0, 2)
+    for copy in smalls:
+        copy.wait()
+    probe_wide[...] = dot(probe_ref[...], spread, ((0,), (0,))).astype(bf16)
     lengths = lengths_ref[...].astype(f32)
     of_group = iota((crop_groups, crops), 1) // pack == iota((crop_groups, crops), 0)
     to_lane = (iota((crops, lanes), 0) % pack == iota((crops, lanes), 1) % pack).astype(bf16)
@@ -177,52 +218,51 @@
 
     text_copies = share_loop(text_all, text_send, text_recv)
 
-    def pool_group(rows, valid, place):
-        scores = dot(rows, probe_wide[...]) * (1.0 / math.sqrt(head_dim))
-        masked = jnp.where(valid, scores, very_low)
-        peak = jnp.max(masked, axis=0, keepdims=True)
-        weight = jnp.exp(masked - peak)
-        total = jnp.sum(weight, axis=0, keepdims=True)
-        part = pl.ds(place, pack)
-        peak_rows[part, :] = jnp.broadcast_to(peak, (pack, lanes))
-        total_rows[part, :] = jnp.broadcast_to(total, (pack, lanes))
-        summed = dot(weight.astype(bf16), rows, ((0,), (0,)))
-        return summed.reshape(heads, pack, width)
+    def pool_pair(pair, valid, places):
+        scores = [dot(rows, probe_wide[...]) * (1.0 / math.sqrt(head_dim)) for rows in pair]
+        found = []
+        for rows, score, keep, place in zip(pair, scores, valid, places):
+            masked = jnp.where(keep, score, very_low)
+            peak = jnp.max(masked, axis=0, keepdims=True)
+            weight = jnp.exp(masked - peak)
+            total = jnp.sum(weight, axis=0, keepdims=True)
+            part = pl.ds(place, pack)
+            peak_rows[part, :] = jnp.broadcast_to(peak, (pack, lanes))
+            total_rows[part, :] = jnp.broadcast_to(total, (pack, lanes))
+            summed = dot(weight.astype(bf16), rows, ((0,), (0,)))
+            found.append(summed.reshape(heads, pack, width))
+        return jnp.concatenate(found, axis=1).astype(bf16)
 
     def crop_pair(i, carry):
-        found = []
-        for half in range(2):
-            g = 2 * i + half
+        groups = (2 * i, 2 * i + 1)
+        for g in groups:
             load_crops(g).wait()
-            rows = tokens[pl.ds(g * pack, pack)].reshape(pack * crop_tok, width)
-            valid = crop_key[...] < len_rows[pl.ds(g, 1), :]
-            found.append(pool_group(rows, valid, pl.multiple_of(g * pack, pack)))
+        pair = [tokens[pl.ds(g * pack, pack)].reshape(pack * crop_tok, width) for g in groups]
+        valid = [crop_key[...] < len_rows[pl.ds(g, 1), :] for g in groups]
+        places = [pl.multiple_of(g * pack, pack) for g in groups]
         place = pl.ds(pl.multiple_of(i * 2 * pack, 2 * pack), 2 * pack)
-        mixed[:, place, :] = jnp.concatenate(found, axis=1).astype(bf16)
+        mixed[:, place, :] = pool_pair(pair, valid, places)
         return carry
 
     lax.fori_loop(0, crop_groups // 2, crop_pair, 0)
 
-    def project(first, count, store):
-        for c0 in range(0, width, 256):
-            w = min(256, width - c0)
-            h0, h1 = c0 // head_dim, (c0 + w - 1) // head_dim + 1
+    def project(first, count, c0, c1, store):
+        for b0 in range(c0, c1, 256):
+            w = min(256, c1 - b0)
+            h0, h1 = b0 // head_dim, (b0 + w - 1) // head_dim + 1
             rows = mixed[h0:h1, first : first + count, :].reshape((h1 - h0) * count, width)
-            block = dot(rows, value[:, c0 : c0 + w]).reshape(h1 - h0, count, w)
-            head_of = (iota((1, w), 1) + c0) // head_dim
+            block = dot(rows, value[:, b0 : b0 + w]).reshape(h1 - h0, count, w)
+            head_of = (iota((1, w), 1) + b0) // head_dim
             kept = jnp.where(head_of == h0, block[0], 0.0)
             for h in range(h0 + 1, h1):
                 kept = jnp.where(head_of == h, block[h - h0], kept)
-            store(c0, w, kept)
-
-    def store_crop(c0, w, block):
-        shares[:, c0 : c0 + w] = block.astype(bf16)
-
-    def store_base(c0, w, block):
-        base_sum[:, c0 : c0 + w] = block
-
-    load_value.wait()
-    project(0, crops, store_crop)
+            store(b0, w, kept)
+
+    def store_crop(b0, w, block):
+        shares[:, b0 : b0 + w] = block.astype(bf16)
+
+    def store_base(b0, w, block):
+        base_sum[:, b0 : b0 + w] = block
 
     def by_crop(rows_ref, first, count):
         keep = iota((count, lanes), 0) % pack == iota((count, lanes), 1) % pack
@@ -239,46 +279,59 @@
     slot_column = to_column(slot_ref[...].astype(f32))
     meta_lane = iota((crops, meta_width), 1)
     meta = jnp.where(meta_lane == n_pieces * heads, slot_column + 1.0, meta)
-    shares[:, width:] = meta.astype(bf16)
-
-    owner_column = owner_ref[...].astype(f32)
-    owner_row = to_row(owner_column)
+
+    owner_row = owner_ref[...].astype(f32)
+    owner_column = to_column(owner_row)
     earlier = (owner_column == owner_row) & (iota((crops, crops), 0) < iota((crops, crops), 1))
     rank = jnp.sum(jnp.where(earlier, 1.0, 0.0), axis=0, keepdims=True)
     target = (owner_row * cap + rank).astype(jnp.int32)
     chosen = (iota((slots, crops), 0) == target).astype(bf16)
-    send[...] = dot(chosen, shares[...]).astype(bf16).reshape(owners, cap, wide)
-
-    crop_copies = []
-    for k in range(1, owners):
-        peer = lax.rem(me + k, owners)
-        copy = pltpu.make_async_remote_copy(
-            src_ref=send.at[peer],
-            dst_ref=recv.at[me],
-            send_sem=crop_send.at[k],
-            recv_sem=crop_recv.at[k],
+
+    def crop_copy(n, sent, held, k, peer, place):
+        return pltpu.make_async_remote_copy(
+            src_ref=sent.at[peer],
+            dst_ref=held.at[place],
+            send_sem=crop_send.at[n, k],
+            recv_sem=crop_recv.at[n, k],
             device_id=(peer, my_loop),
             device_id_type=MESH,
         )
-        copy.start()
-        crop_copies.append(copy)
-    recv[me] = send[me]
+
+    crop_copies = []
+
+    def share_crops(n, sent, held, rows):
+        sent[...] = dot(chosen, rows).astype(bf16).reshape(sent.shape)
+        for k in range(1, owners):
+            copy = crop_copy(n, sent, held, k, lax.rem(me + k, owners), me)
+            copy.start()
+            crop_copies.append(copy)
+        held[me] = sent[me]
+
+    def await_crops(n, sent, held):
+        for k in range(1, owners):
+            source = lax.rem(me + owners - k, owners)
+            crop_copy(n, sent, held, k, source, source).wait_recv()
+
+    share_crops(0, meta_send, meta_recv, meta.astype(bf16))
+    load_value.wait()
+    chunks = column_chunks(width)
+    buffers = [(send_0, recv_0), (send_1, recv_1), (send_2, recv_2)]
+    for n, (c0, c1) in enumerate(chunks):
+        project(0, crops, c0, c1, store_crop)
+        share_crops(n + 1, *buffers[n], shares[:, c0:c1])
 
     load_base.wait()
 
     def base_pair(i, carry):
-        found = []
-        for half in range(2):
-            g = 2 * i + half
-            rows = base[pl.ds(g * pack, pack)].reshape(pack * base_tok, width)
-            place = pl.multiple_of(crops + g * pack, pack)
-            found.append(pool_group(rows, base_key[...] < 1, place))
+        groups = (2 * i, 2 * i + 1)
+        pair = [base[pl.ds(g * pack, pack)].reshape(pack * base_tok, width) for g in groups]
+        places = [pl.multiple_of(crops + g * pack, pack) for g in groups]
         place = pl.ds(pl.multiple_of(crops + i * 2 * pack, 2 * pack), 2 * pack)
-        mixed[:, place, :] = jnp.concatenate(found, axis=1).astype(bf16)
+        mixed[:, place, :] = pool_pair(pair, [base_key[...] < 1] * 2, places)
         return carry
 
     lax.fori_loop(0, base_groups // 2, base_pair, 0)
-    project(crops, images, store_base)
+    project(crops, images, 0, width, store_base)
     fold = (iota((lanes, heads), 0) // pack == iota((lanes, heads), 1)).astype(bf16)
 
     def folded(x):
@@ -286,22 +339,9 @@
 
     base_peak = folded(by_crop(peak_rows, crops, images))
     base_total = folded(by_crop(total_rows, crops, images))
-    load_out.wait()
-    await_loop(text_all, text_send, text_recv)
-
-    for k in range(1, owners):
-        source = lax.rem(me + owners - k, owners)
-        pltpu.make_async_remote_copy(
-            src_ref=send.at[source],
-            dst_ref=recv.at[source],
-            send_sem=crop_send.at[k],
-            recv_sem=crop_recv.at[k],
-            device_id=(source, my_loop),
-            device_id_type=MESH,
-        ).wait_recv()
-
-    arrived = recv[...].reshape(slots, wide)
-    meta = arrived[:, width:]
+    await_crops(0, meta_send, meta_recv)
+
+    meta = meta_recv[...].reshape(slots, meta_width)
     m_row, m_col = iota((meta_width, meta_width), 0), iota((meta_width, meta_width), 1)
     is_peak = (m_row < 3 * heads) & (m_row % heads == m_col)
     is_total = (m_row >= 3 * heads) & (m_row < 6 * heads) & (m_row % heads + heads == m_col)
@@ -329,12 +369,17 @@
     inverse = 1.0 / (base_total * base_rescale + collected)
     inverse_at = sum(dot(member_b, piece) for piece in split(inverse, 2))
     widen = (iota((heads, width), 1) // head_dim == iota((heads, width), 0)).astype(bf16)
-    crop_factor = sum(dot(piece, widen) for piece in split(rescale * inverse_at, 2))
-    base_factor = sum(dot(piece, widen) for piece in split(base_rescale * inverse, 2))
-    scaled = arrived[:, :width].astype(f32) * crop_factor
-    merged = sum(dot(member_tb, piece) for piece in split(scaled, 2))
-    pooled = (base_sum[...] * base_factor + merged).astype(bf16)
-    features = dot(pooled, outw[...])
+    crop_factor[...] = sum(dot(piece, widen) for piece in split(rescale * inverse_at, 2))
+    base_factor[...] = sum(dot(piece, widen) for piece in split(base_rescale * inverse, 2))
+    load_out.wait()
+    await_loop(text_all, text_send, text_recv)
+    features = jnp.zeros((images, width), f32)
+    for n, (c0, c1) in enumerate(chunks):
+        await_crops(n + 1, *buffers[n])
+        arrived = buffers[n][1][...].reshape(slots, c1 - c0).astype(f32)
+        scaled = (arrived * crop_factor[:, c0:c1]).astype(bf16)
+        pooled = base_sum[:, c0:c1] * base_factor[:, c0:c1] + dot(member_tb, scaled)
+        features += dot(pooled.astype(bf16), outw[c0:c1, :])
     embed_ref[...] = features.astype(bf16)
     image_all[my_loop] = unit_rows(features)
     image_copies = share_loop(image_all, image_send, image_recv)
@@ -359,6 +404,19 @@
     )
     for copy in text_copies + crop_copies + image_copies:
         copy.wait_send()
+
+
+def hand_over(embed, image_grad, text_grad, embed_out, image_out, text_out, sem):
+    copies = [
+        pltpu.make_async_copy(source, held, sem.at[i])
+        for i, (source, held) in enumerate(
+            [(image_grad, image_out), (text_grad, text_out), (embed, embed_out)]
+        )
+    ]
+    for copy in copies:
+        copy.start()
+    for copy in copies:
+        copy.wait()
 
 
 def per_device(
@@ -385,21 +443,30 @@
     cap = -(-cap // 16) * 16
     wide = width + 128
     groups = crops // pack
+    chunk_buffers = [
+        pltpu.VMEM((owners, cap, c1 - c0), bf16) for c0, c1 in column_chunks(width)
+    ]
     vmem = pl.BlockSpec(memory_space=pltpu.VMEM)
     smem = pl.BlockSpec(memory_space=pltpu.SMEM)
     hbm = pl.BlockSpec(memory_space=pl.ANY)
     flops = 2 * (crops * crop_tok + images * base_tok) * width * heads * 2
     flops += 2 * (crops + 2 * images) * width * width
-    return pl.pallas_call(
+    step = pl.pallas_call(
         functools.partial(step_kernel, (owners, loops, cap)),
         out_shape=(
             jax.ShapeDtypeStruct((images, width), bf16),
             jax.ShapeDtypeStruct((images, width), f32),
             jax.ShapeDtypeStruct((images, width), f32),
         ),
-        in_specs=[vmem] * 6 + [smem] * 2 + [hbm] * 4,
+        in_specs=[hbm] * 6 + [smem] * 2 + [hbm] * 4,
         out_specs=(vmem, vmem, vmem),
         scratch_shapes=[
+            pltpu.VMEM((1, crops), jnp.int32),
+            pltpu.VMEM((1, crops), jnp.int32),
+            pltpu.VMEM((1, crops), jnp.int32),
+            pltpu.VMEM((heads, width), bf16),
+            pltpu.VMEM((images, width), bf16),
+            pltpu.VMEM((1, images), jnp.int32),
             pltpu.VMEM(crop_tokens.shape, bf16),
             pltpu.VMEM(base_tokens.shape, bf16),
             pltpu.VMEM((width, width), bf16),
@@ -411,17 +478,22 @@
             pltpu.VMEM((heads, crops + images, width), bf16),
             pltpu.VMEM((crops + images, lanes), f32),
             pltpu.VMEM((crops + images, lanes), f32),
-            pltpu.VMEM((crops, wide), bf16),
+            pltpu.VMEM((crops, width), bf16),
             pltpu.VMEM((images, width), f32),
-            pltpu.VMEM((owners, cap, wide), bf16),
-            pltpu.VMEM((owners, cap, wide), bf16),
+            pltpu.VMEM((owners * cap, width), f32),
+            pltpu.VMEM((images, width), f32),
+            pltpu.VMEM((owners, cap, wide - width), bf16),
+            pltpu.VMEM((owners, cap, wide - width), bf16),
+            *chunk_buffers,
+            *chunk_buffers,
             pltpu.VMEM((loops, images, wide), bf16),
             pltpu.VMEM((loops, images, width), bf16),
             pltpu.SemaphoreType.DMA((groups + 3,)),
+            pltpu.SemaphoreType.DMA((6,)),
             pltpu.SemaphoreType.DMA((loops,)),
             pltpu.SemaphoreType.DMA((loops,)),
-            pltpu.SemaphoreType.DMA((owners,)),
-            pltpu.SemaphoreType.DMA((owners,)),
+            pltpu.SemaphoreType.DMA((len(chunk_buffers) + 1, owners)),
+            pltpu.SemaphoreType.DMA((len(chunk_buffers) + 1, owners)),
             pltpu.SemaphoreType.DMA((loops,)),
             pltpu.SemaphoreType.DMA((loops,)),
         ],
@@ -432,11 +504,12 @@
             flops=flops, bytes_accessed=17 * 1024 * 1024, transcendentals=0
         ),
         name="contrastive_step",
-    )(
+    )
+    results = step(
         crop_lengths,
-        crop_owner,
+        crop_owner.reshape(1, crops),
         crop_slot.reshape(1, crops),
-        key_probe,
+        key_probe.T,
         text_embed,
         pair_labels.reshape(1, images),
         logit_scale,
@@ -446,6 +519,15 @@
         value_weight,
         out_weight,
     )
+    return pl.pallas_call(
+        hand_over,
+        out_shape=tuple(jax.ShapeDtypeStruct(r.shape, r.dtype) for r in results),
+        in_specs=[hbm] * 3,
+        out_specs=(hbm, hbm, hbm),
+        scratch_shapes=[pltpu.SemaphoreType.DMA((3,))],
+        compiler_params=pltpu.CompilerParams(vmem_limit_bytes=56 * 1024 * 1024),
+        name="hand_over",
+    )(*results)
 
 
 def solution(mesh):

time: 43.1 us -> 45.6 us (1.058)
  Pallas kernels: 33.2 us -> 43.5 us
  local copies, waits for them, and re-layouts: 7.69 us -> 0 us
    pallas_call x1 -> x2, Pallas kernels: 33.2 us -> 43.5 us  [the longest x1 31.2 us: per_device(): step(crop_lengths, crop_owner.reshape(1, crops), crop_slot.reshape(1, cro...]
    unnamed x5 -> x0, local copies, waits for them, and re-layouts: 7.69 us -> none
where the time goes in v2:
time: 45.6 us; the launch traced here: 45.5 us
  Pallas kernels  43.5 us (95%)
  between operations  1.93 us (4%)
    pallas_call x1, Pallas kernels, per_device(): step(crop_lengths, crop_owner.reshape(1, crops), crop_slot.reshape(1, cro...  31.2 us
    pallas_call x1, Pallas kernels, per_device(): pl.pallas_call(hand_over, out_shape=tuple((jax.ShapeDtypeStruct(r.shape,...  12.3 us

profile of v2, /device:TPU:0, one launch (start us, length us, event | category | flops | bytes accessed | tf_op | source)
XLA Modules:
  0.0 45.5 jit_solution(12709741128431232421)
XLA Ops:
  1.9 31.2 %contrastive_step.1 = (bf16[32,1152]{1,0:T(8,128)(2,1)}, f32[32,1152]{1,0:T(8,128)}, f32[32,1152]{1,0:T(8,128)}) custom-call(s32[1,64]{1,0:T(1,128)} %lengths_hbm.1, s32[1,64]{1,0:T(1,128)} %bitcast.5, s32[1,64]{1,0:T(1,128)} %bitcast.6, bf16[16,1152]{1,0:T(8,128)(2,1)} %bitcast.4, bf16[32,1152]{1,0:T(8,128)(2,1)} %text_hbm.1, s32[1,32]{1,0:T(1,128)} %bitcast.7, ...), custom_call_target="tpu_custom_call" | custom-call | flops 717225984 | bytes 17825792 | tf_op jit(solution)/shard_map/contrastive_step/pallas_call | solution.py:508
  33.2 12.3 %hand_over.1 = (bf16[32,1152]{1,0:T(8,128)(2,1)}, f32[32,1152]{1,0:T(8,128)}, f32[32,1152]{1,0:T(8,128)}) custom-call(bf16[32,1152]{1,0:T(8,128)(2,1)} %get-tuple-element.6.embed, f32[32,1152]{1,0:T(8,128)} %get-tuple-element.7.image_grad, f32[32,1152]{1,0:T(8,128)} %get-tuple-element.8.text_grad), custom_call_target="tpu_custom_call" | custom-call | tf_op jit(solution)/shard_map/hand_over/pallas_call | solution.py:522

commit v3 on v2

--- a/solution.py
+++ b/solution.py
@@ -83,13 +83,11 @@
     base,
     value,
     outw,
-    probe_wide,
     crop_key,
-    base_key,
     len_rows,
     mixed,
-    peak_rows,
-    total_rows,
+    peak_cols,
+    total_cols,
     shares,
     base_sum,
     crop_factor,
@@ -167,27 +165,21 @@
     load_base.start()
     load_out.start()
 
-    spread = (iota((heads, lanes), 1) // pack == iota((heads, lanes), 0)).astype(bf16)
-    lane_of = iota((1, lanes), 1) % pack
-    row = iota((pack * crop_tok, lanes), 0)
-    crop_key[...] = jnp.where(row // crop_tok == lane_of, row % crop_tok, 2 * crop_tok)
-    row = iota((pack * base_tok, lanes), 0)
-    base_key[...] = jnp.where(row // base_tok == lane_of, 0, 2)
+    column = iota((pack, pack * crop_tok), 1)
+    mine = iota((pack, pack * crop_tok), 0) == column // crop_tok
+    crop_key[...] = jnp.where(mine, column % crop_tok, 2 * crop_tok)
+    base_key = iota((pack, pack * base_tok), 0) == iota((pack, pack * base_tok), 1) // base_tok
     for copy in smalls:
         copy.wait()
-    probe_wide[...] = dot(probe_ref[...], spread, ((0,), (0,))).astype(bf16)
-    lengths = lengths_ref[...].astype(f32)
-    of_group = iota((crop_groups, crops), 1) // pack == iota((crop_groups, crops), 0)
-    to_lane = (iota((crops, lanes), 0) % pack == iota((crops, lanes), 1) % pack).astype(bf16)
-    len_rows[...] = dot(jnp.where(of_group, lengths, 0.0).astype(bf16), to_lane).astype(jnp.int32)
+    len_rows[...] = jnp.broadcast_to(to_column(lengths_ref[...].astype(f32)), len_rows.shape)
+    peak_cols[...] = jnp.zeros_like(peak_cols)
+    total_cols[...] = jnp.zeros_like(total_cols)
 
     text_unit = unit_rows(text_ref[...].astype(f32))
     labels = labels_ref[...].astype(f32)
     label_block = jnp.broadcast_to(to_column(labels), (images, wide - width)).astype(bf16)
     text_all[my_loop, :, :width] = text_unit
     text_all[my_loop, :, width:] = label_block
-
-    pl.semaphore_wait(barrier, owners - 1 + loops - 1)
 
     def share_loop(buffer, send_sem, recv_sem):
         copies = []
@@ -216,21 +208,23 @@
                 device_id_type=MESH,
             ).wait_recv()
 
-    text_copies = share_loop(text_all, text_send, text_recv)
-
-    def pool_pair(pair, valid, places):
-        scores = [dot(rows, probe_wide[...]) * (1.0 / math.sqrt(head_dim)) for rows in pair]
+    def pool_pair(pair, valid, groups):
+        scores = [
+            dot(probe_ref[...], rows, ((1,), (1,))) * (1.0 / math.sqrt(head_dim)) for rows in pair
+        ]
         found = []
-        for rows, score, keep, place in zip(pair, scores, valid, places):
-            masked = jnp.where(keep, score, very_low)
-            peak = jnp.max(masked, axis=0, keepdims=True)
+        for rows, score, keep, g in zip(pair, scores, valid, groups):
+            shape = (heads,) + keep.shape
+            copied = jnp.broadcast_to(score[:, None, :], shape)
+            masked = jnp.where(jnp.broadcast_to(keep[None], shape), copied, very_low)
+            masked = masked.reshape(lanes, keep.shape[1])
+            peak = jnp.max(masked, axis=1, keepdims=True)
             weight = jnp.exp(masked - peak)
-            total = jnp.sum(weight, axis=0, keepdims=True)
-            part = pl.ds(place, pack)
-            peak_rows[part, :] = jnp.broadcast_to(peak, (pack, lanes))
-            total_rows[part, :] = jnp.broadcast_to(total, (pack, lanes))
-            summed = dot(weight.astype(bf16), rows, ((0,), (0,)))
-            found.append(summed.reshape(heads, pack, width))
+            total = jnp.sum(weight, axis=1, keepdims=True)
+            at = iota((lanes, lanes), 1) == g
+            peak_cols[...] = jnp.where(at, peak, peak_cols[...])
+            total_cols[...] = jnp.where(at, total, total_cols[...])
+            found.append(dot(weight.astype(bf16), rows).reshape(heads, pack, width))
         return jnp.concatenate(found, axis=1).astype(bf16)
 
     def crop_pair(i, carry):
@@ -238,13 +232,16 @@
         for g in groups:
             load_crops(g).wait()
         pair = [tokens[pl.ds(g * pack, pack)].reshape(pack * crop_tok, width) for g in groups]
-        valid = [crop_key[...] < len_rows[pl.ds(g, 1), :] for g in groups]
-        places = [pl.multiple_of(g * pack, pack) for g in groups]
+        valid = []
+        for g in groups:
+            length = len_rows[pl.ds(pl.multiple_of(g * pack, pack), pack), :]
+            valid.append(crop_key[...].astype(f32) < length[:, :1])
         place = pl.ds(pl.multiple_of(i * 2 * pack, 2 * pack), 2 * pack)
-        mixed[:, place, :] = pool_pair(pair, valid, places)
+        mixed[:, place, :] = pool_pair(pair, valid, groups)
         return carry
 
     lax.fori_loop(0, crop_groups // 2, crop_pair, 0)
+    pl.semaphore_wait(barrier, owners - 1 + loops - 1)
 
     def project(first, count, c0, c1, store):
         for b0 in range(c0, c1, 256):
@@ -264,12 +261,14 @@
     def store_base(b0, w, block):
         base_sum[:, b0 : b0 + w] = block
 
-    def by_crop(rows_ref, first, count):
+    def by_crop(columns_ref, first, count):
+        rows = columns_ref[...].T[first // pack : (first + count) // pack, :]
+        rows = jnp.broadcast_to(rows[:, None, :], (count // pack, pack, lanes))
         keep = iota((count, lanes), 0) % pack == iota((count, lanes), 1) % pack
-        return jnp.where(keep, rows_ref[first : first + count, :], 0.0)
+        return jnp.where(keep, rows.reshape(count, lanes), 0.0)
 
     meta_width = wide - width
-    pieces = split(by_crop(peak_rows, 0, crops), 3) + split(by_crop(total_rows, 0, crops), 3)
+    pieces = split(by_crop(peak_cols, 0, crops), 3) + split(by_crop(total_cols, 0, crops), 3)
     n_pieces = len(pieces)
     k_index = iota((n_pieces * lanes, meta_width), 0)
     gather = k_index // lanes * heads + k_index % lanes // pack == iota(
@@ -320,14 +319,17 @@
         project(0, crops, c0, c1, store_crop)
         share_crops(n + 1, *buffers[n], shares[:, c0:c1])
 
+    text_copies = share_loop(text_all, text_send, text_recv)
+
     load_base.wait()
 
     def base_pair(i, carry):
         groups = (2 * i, 2 * i + 1)
         pair = [base[pl.ds(g * pack, pack)].reshape(pack * base_tok, width) for g in groups]
-        places = [pl.multiple_of(crops + g * pack, pack) for g in groups]
         place = pl.ds(pl.multiple_of(crops + i * 2 * pack, 2 * pack), 2 * pack)
-        mixed[:, place, :] = pool_pair(pair, [base_key[...] < 1] * 2, places)
+        mixed[:, place, :] = pool_pair(
+            pair, [base_key] * 2, [crop_groups + g for g in groups]
+        )
         return carry
 
     lax.fori_loop(0, base_groups // 2, base_pair, 0)
@@ -337,8 +339,8 @@
     def folded(x):
         return sum(dot(piece, fold) for piece in split(x, 3))
 
-    base_peak = folded(by_crop(peak_rows, crops, images))
-    base_total = folded(by_crop(total_rows, crops, images))
+    base_peak = folded(by_crop(peak_cols, crops, images))
+    base_total = folded(by_crop(total_cols, crops, images))
     await_crops(0, meta_send, meta_recv)
 
     meta = meta_recv[...].reshape(slots, meta_width)
@@ -406,17 +408,10 @@
         copy.wait_send()
 
 
-def hand_over(embed, image_grad, text_grad, embed_out, image_out, text_out, sem):
-    copies = [
-        pltpu.make_async_copy(source, held, sem.at[i])
-        for i, (source, held) in enumerate(
-            [(image_grad, image_out), (text_grad, text_out), (embed, embed_out)]
-        )
-    ]
-    for copy in copies:
-        copy.start()
-    for copy in copies:
-        copy.wait()
+def hand_over(embed, image_grad, text_grad, embed_out, image_out, text_out):
+    embed_out[...] = embed[...]
+    image_out[...] = image_grad[...]
+    text_out[...] = text_grad[...]
 
 
 def per_device(
@@ -471,13 +466,11 @@
             pltpu.VMEM(base_tokens.shape, bf16),
             pltpu.VMEM((width, width), bf16),
             pltpu.VMEM((width, width), bf16),
-            pltpu.VMEM((width, lanes), bf16),
-            pltpu.VMEM((pack * crop_tok, lanes), jnp.int32),
-            pltpu.VMEM((pack * base_tok, lanes), jnp.int32),
-            pltpu.VMEM((groups, lanes), jnp.int32),
+            pltpu.VMEM((pack, pack * crop_tok), jnp.int32),
+            pltpu.VMEM((crops, 128), f32),
             pltpu.VMEM((heads, crops + images, width), bf16),
-            pltpu.VMEM((crops + images, lanes), f32),
-            pltpu.VMEM((crops + images, lanes), f32),
+            pltpu.VMEM((lanes, lanes), f32),
+            pltpu.VMEM((lanes, lanes), f32),
             pltpu.VMEM((crops, width), bf16),
             pltpu.VMEM((images, width), f32),
             pltpu.VMEM((owners * cap, width), f32),
@@ -522,9 +515,8 @@
     return pl.pallas_call(
         hand_over,
         out_shape=tuple(jax.ShapeDtypeStruct(r.shape, r.dtype) for r in results),
-        in_specs=[hbm] * 3,
-        out_specs=(hbm, hbm, hbm),
-        scratch_shapes=[pltpu.SemaphoreType.DMA((3,))],
+        in_specs=[vmem] * 3,
+        out_specs=(vmem, vmem, vmem),
         compiler_params=pltpu.CompilerParams(vmem_limit_bytes=56 * 1024 * 1024),
         name="hand_over",
     )(*results)

time: 45.6 us -> 34.4 us (0.75)
  Pallas kernels: 43.5 us -> 32.3 us
    pallas_call x1, Pallas kernels: 12.3 us -> 1.76 us  [per_device(): pl.pallas_call(hand_over, out_shape=tuple((jax.ShapeDtypeStruct(r.shape,...]
    pallas_call x1, Pallas kernels: 31.2 us -> 30.5 us  [per_device(): step(crop_lengths, crop_owner.reshape(1, crops), crop_slot.reshape(1, cro...]
where the time goes in v3:
time: 34.4 us; the launch traced here: 34.2 us
  Pallas kernels  32.3 us (94%)
  between operations  1.93 us (6%)
    pallas_call x1, Pallas kernels, per_device(): step(crop_lengths, crop_owner.reshape(1, crops), crop_slot.reshape(1, cro...  30.5 us
    pallas_call x1, Pallas kernels, per_device(): pl.pallas_call(hand_over, out_shape=tuple((jax.ShapeDtypeStruct(r.shape,...  1.76 us

profile of v3, /device:TPU:0, one launch (start us, length us, event | category | flops | bytes accessed | tf_op | source)
XLA Modules:
  0.0 34.2 jit_solution(6895443014935416819)
XLA Ops:
  1.9 30.5 %contrastive_step.1 = (bf16[32,1152]{1,0:T(8,128)(2,1)}, f32[32,1152]{1,0:T(8,128)}, f32[32,1152]{1,0:T(8,128)}) custom-call(s32[1,64]{1,0:T(1,128)} %lengths_hbm.1, s32[1,64]{1,0:T(1,128)} %bitcast.5, s32[1,64]{1,0:T(1,128)} %bitcast.6, bf16[16,1152]{1,0:T(8,128)(2,1)} %bitcast.4, bf16[32,1152]{1,0:T(8,128)(2,1)} %text_hbm.1, s32[1,32]{1,0:T(1,128)} %bitcast.7, ...), custom_call_target="tpu_custom_call" | custom-call | flops 717225984 | bytes 17825792 | tf_op jit(solution)/shard_map/contrastive_step/pallas_call | solution.py:501
  32.4 1.8 %hand_over.1 = (bf16[32,1152]{1,0:T(8,128)(2,1)}, f32[32,1152]{1,0:T(8,128)}, f32[32,1152]{1,0:T(8,128)}) custom-call(bf16[32,1152]{1,0:T(8,128)(2,1)} %get-tuple-element.6.embed, f32[32,1152]{1,0:T(8,128)} %get-tuple-element.7.image_grad, f32[32,1152]{1,0:T(8,128)} %get-tuple-element.8.text_grad), custom_call_target="tpu_custom_call" | custom-call | tf_op jit(solution)/shard_map/hand_over/pallas_call | solution.py:515

commit v4 on v3

--- a/solution.py
+++ b/solution.py
@@ -50,10 +50,10 @@
     return (matrix * lax.rsqrt(total + norm_eps)).astype(bf16)
 
 
-def column_chunks(width):
-    first = min(256, width)
-    middle = max(first, (2 * width // 3) // 256 * 256)
-    return [(0, first), (first, middle), (middle, width)]
+def column_chunks(width, heads):
+    first = (heads // 2) * (width // heads) // 256 * 256
+    last = max(first, width - 256)
+    return [(0, first), (first, last), (last, width)]
 
 
 def step_kernel(
@@ -101,15 +101,16 @@
     recv_1,
     recv_2,
     text_all,
-    image_all,
+    pooled_0,
+    pooled_1,
+    pooled_2,
+    weights,
     load_sem,
     small_sem,
-    text_send,
-    text_recv,
+    loop_send,
+    loop_recv,
     crop_send,
     crop_recv,
-    image_send,
-    image_recv,
 ):
     owners, loops, cap = dims
     crops, crop_tok, width = tokens.shape
@@ -181,32 +182,29 @@
     text_all[my_loop, :, :width] = text_unit
     text_all[my_loop, :, width:] = label_block
 
-    def share_loop(buffer, send_sem, recv_sem):
-        copies = []
+    def loop_copy(buffer, send_sem, recv_sem, peer, place):
+        return pltpu.make_async_remote_copy(
+            src_ref=buffer.at[place],
+            dst_ref=buffer.at[place],
+            send_sem=send_sem,
+            recv_sem=recv_sem,
+            device_id=(me, peer),
+            device_id_type=MESH,
+        )
+
+    loop_copies = []
+
+    def share_loop(n, buffer):
         for k in range(1, loops):
-            copy = pltpu.make_async_remote_copy(
-                src_ref=buffer.at[my_loop],
-                dst_ref=buffer.at[my_loop],
-                send_sem=send_sem.at[k],
-                recv_sem=recv_sem.at[k],
-                device_id=(me, lax.rem(my_loop + k, loops)),
-                device_id_type=MESH,
-            )
+            peer = lax.rem(my_loop + k, loops)
+            copy = loop_copy(buffer, loop_send.at[n, k], loop_recv.at[n, k], peer, my_loop)
             copy.start()
-            copies.append(copy)
-        return copies
-
-    def await_loop(buffer, send_sem, recv_sem):
+            loop_copies.append(copy)
+
+    def await_loop(n, buffer):
         for k in range(1, loops):
             source = lax.rem(my_loop + loops - k, loops)
-            pltpu.make_async_remote_copy(
-                src_ref=buffer.at[source],
-                dst_ref=buffer.at[source],
-                send_sem=send_sem.at[k],
-                recv_sem=recv_sem.at[k],
-                device_id=(me, source),
-                device_id_type=MESH,
-            ).wait_recv()
+            loop_copy(buffer, loop_send.at[n, k], loop_recv.at[n, k], source, source).wait_recv()
 
     def pool_pair(pair, valid, groups):
         scores = [
@@ -224,8 +222,17 @@
             at = iota((lanes, lanes), 1) == g
             peak_cols[...] = jnp.where(at, peak, peak_cols[...])
             total_cols[...] = jnp.where(at, total, total_cols[...])
-            found.append(dot(weight.astype(bf16), rows).reshape(heads, pack, width))
-        return jnp.concatenate(found, axis=1).astype(bf16)
+            found.append(weight.astype(bf16))
+        return found
+
+    def mix_pair(pair, weight, place, h0, h1):
+        found = [
+            dot(part[h0 * pack : h1 * pack], rows).reshape(h1 - h0, pack, width)
+            for part, rows in zip(weight, pair)
+        ]
+        mixed[h0:h1, place, :] = jnp.concatenate(found, axis=1).astype(bf16)
+
+    half = heads // 2
 
     def crop_pair(i, carry):
         groups = (2 * i, 2 * i + 1)
@@ -237,7 +244,21 @@
             length = len_rows[pl.ds(pl.multiple_of(g * pack, pack), pack), :]
             valid.append(crop_key[...].astype(f32) < length[:, :1])
         place = pl.ds(pl.multiple_of(i * 2 * pack, 2 * pack), 2 * pack)
-        mixed[:, place, :] = pool_pair(pair, valid, groups)
+        weight = pool_pair(pair, valid, groups)
+        for g, part in zip(groups, weight):
+            weights[g] = part[half * pack :]
+        mix_pair(pair, weight, place, 0, half)
+        return carry
+
+    def crop_pair_rest(i, carry):
+        groups = (2 * i, 2 * i + 1)
+        pair = [tokens[pl.ds(g * pack, pack)].reshape(pack * crop_tok, width) for g in groups]
+        place = pl.ds(pl.multiple_of(i * 2 * pack, 2 * pack), 2 * pack)
+        found = [
+            dot(weights[g], rows).reshape(heads - half, pack, width)
+            for g, rows in zip(groups, pair)
+        ]
+        mixed[half:, place, :] = jnp.concatenate(found, axis=1).astype(bf16)
         return carry
 
     lax.fori_loop(0, crop_groups // 2, crop_pair, 0)
@@ -313,13 +334,15 @@
 
     share_crops(0, meta_send, meta_recv, meta.astype(bf16))
     load_value.wait()
-    chunks = column_chunks(width)
+    chunks = column_chunks(width, heads)
     buffers = [(send_0, recv_0), (send_1, recv_1), (send_2, recv_2)]
     for n, (c0, c1) in enumerate(chunks):
+        if n == 1:
+            lax.fori_loop(0, crop_groups // 2, crop_pair_rest, 0)
         project(0, crops, c0, c1, store_crop)
         share_crops(n + 1, *buffers[n], shares[:, c0:c1])
 
-    text_copies = share_loop(text_all, text_send, text_recv)
+    share_loop(0, text_all)
 
     load_base.wait()
 
@@ -327,9 +350,8 @@
         groups = (2 * i, 2 * i + 1)
         pair = [base[pl.ds(g * pack, pack)].reshape(pack * base_tok, width) for g in groups]
         place = pl.ds(pl.multiple_of(crops + i * 2 * pack, 2 * pack), 2 * pack)
-        mixed[:, place, :] = pool_pair(
-            pair, [base_key] * 2, [crop_groups + g for g in groups]
-        )
+        weight = pool_pair(pair, [base_key] * 2, [crop_groups + g for g in groups])
+        mix_pair(pair, weight, place, 0, heads)
         return carry
 
     lax.fori_loop(0, base_groups // 2, base_pair, 0)
@@ -374,17 +396,19 @@
     crop_factor[...] = sum(dot(piece, widen) for piece in split(rescale * inverse_at, 2))
     base_factor[...] = sum(dot(piece, widen) for piece in split(base_rescale * inverse, 2))
     load_out.wait()
-    await_loop(text_all, text_send, text_recv)
+    gathered = [pooled_0, pooled_1, pooled_2]
     features = jnp.zeros((images, width), f32)
     for n, (c0, c1) in enumerate(chunks):
         await_crops(n + 1, *buffers[n])
         arrived = buffers[n][1][...].reshape(slots, c1 - c0).astype(f32)
         scaled = (arrived * crop_factor[:, c0:c1]).astype(bf16)
         pooled = base_sum[:, c0:c1] * base_factor[:, c0:c1] + dot(member_tb, scaled)
+        gathered[n][my_loop] = pooled.astype(bf16)
+        share_loop(n + 1, gathered[n])
         features += dot(pooled.astype(bf16), outw[c0:c1, :])
     embed_ref[...] = features.astype(bf16)
-    image_all[my_loop] = unit_rows(features)
-    image_copies = share_loop(image_all, image_send, image_recv)
+    image_unit = unit_rows(features)
+    await_loop(0, text_all)
 
     scale = scale_ref[0]
     bias = bias_ref[0]
@@ -399,12 +423,14 @@
         tile = (scale * (-sign / (1.0 + jnp.exp(sign * logits)))).astype(bf16)
         return dot(tile, others, ((0,), (0,)))
 
-    image_grad_ref[...] = gradient(texts, image_all[my_loop])
-    await_loop(image_all, image_send, image_recv)
-    text_grad_ref[...] = gradient(
-        image_all[...].reshape(group, width), text_all[my_loop, :, :width]
-    )
-    for copy in text_copies + crop_copies + image_copies:
+    image_grad_ref[...] = gradient(texts, image_unit)
+
+    features = jnp.zeros((group, width), f32)
+    for n, (c0, c1) in enumerate(chunks):
+        await_loop(n + 1, gathered[n])
+        features += dot(gathered[n][...].reshape(group, c1 - c0), outw[c0:c1, :])
+    text_grad_ref[...] = gradient(unit_rows(features), text_all[my_loop, :, :width])
+    for copy in loop_copies + crop_copies:
         copy.wait_send()
 
 
@@ -438,8 +464,9 @@
     cap = -(-cap // 16) * 16
     wide = width + 128
     groups = crops // pack
+    chunks = column_chunks(width, heads)
     chunk_buffers = [
-        pltpu.VMEM((owners, cap, c1 - c0), bf16) for c0, c1 in column_chunks(width)
+        pltpu.VMEM((owners, cap, c1 - c0), bf16) for c0, c1 in chunks
     ]
     vmem = pl.BlockSpec(memory_space=pltpu.VMEM)
     smem = pl.BlockSpec(memory_space=pltpu.SMEM)
@@ -480,15 +507,14 @@
             *chunk_buffers,
             *chunk_buffers,
             pltpu.VMEM((loops, images, wide), bf16),
-            pltpu.VMEM((loops, images, width), bf16),
+            *[pltpu.VMEM((loops, images, c1 - c0), bf16) for c0, c1 in chunks],
+            pltpu.VMEM((groups, (heads - heads // 2) * pack, pack * crop_tok), bf16),
             pltpu.SemaphoreType.DMA((groups + 3,)),
             pltpu.SemaphoreType.DMA((6,)),
-            pltpu.SemaphoreType.DMA((loops,)),
-            pltpu.SemaphoreType.DMA((loops,)),
-            pltpu.SemaphoreType.DMA((len(chunk_buffers) + 1, owners)),
-            pltpu.SemaphoreType.DMA((len(chunk_buffers) + 1, owners)),
-            pltpu.SemaphoreType.DMA((loops,)),
-            pltpu.SemaphoreType.DMA((loops,)),
+            pltpu.SemaphoreType.DMA((len(chunks) + 1, loops)),
+            pltpu.SemaphoreType.DMA((len(chunks) + 1, loops)),
+            pltpu.SemaphoreType.DMA((len(chunks) + 1, owners)),
+            pltpu.SemaphoreType.DMA((len(chunks) + 1, owners)),
         ],
         compiler_params=pltpu.CompilerParams(
             collective_id=0, has_side_effects=True, vmem_limit_bytes=56 * 1024 * 1024

time: 34.4 us -> 33.2 us (0.965)
  Pallas kernels: 32.3 us -> 31.1 us
    pallas_call x1, Pallas kernels: 30.5 us -> 29.3 us  [per_device(): step(crop_lengths, crop_owner.reshape(1, crops), crop_slot.reshape(1, cro...]
where the time goes in v4:
time: 33.2 us; the launch traced here: 33 us
  Pallas kernels  31.1 us (94%)
  between operations  1.93 us (6%)
    pallas_call x1, Pallas kernels, per_device(): step(crop_lengths, crop_owner.reshape(1, crops), crop_slot.reshape(1, cro...  29.3 us
    pallas_call x1, Pallas kernels, per_device(): pl.pallas_call(hand_over, out_shape=tuple((jax.ShapeDtypeStruct(r.shape,...  1.76 us

profile of v4, /device:TPU:0, one launch (start us, length us, event | category | flops | bytes accessed | tf_op | source)
XLA Modules:
  0.0 33.0 jit_solution(15434483537638739032)
XLA Ops:
  1.9 29.3 %contrastive_step.1 = (bf16[32,1152]{1,0:T(8,128)(2,1)}, f32[32,1152]{1,0:T(8,128)}, f32[32,1152]{1,0:T(8,128)}) custom-call(s32[1,64]{1,0:T(1,128)} %lengths_hbm.1, s32[1,64]{1,0:T(1,128)} %bitcast.5, s32[1,64]{1,0:T(1,128)} %bitcast.6, bf16[16,1152]{1,0:T(8,128)(2,1)} %bitcast.4, bf16[32,1152]{1,0:T(8,128)(2,1)} %text_hbm.1, s32[1,32]{1,0:T(1,128)} %bitcast.7, ...), custom_call_target="tpu_custom_call" | custom-call | flops 717225984 | bytes 17825792 | tf_op jit(solution)/shard_map/contrastive_step/pallas_call | solution.py:527
  31.3 1.8 %hand_over.1 = (bf16[32,1152]{1,0:T(8,128)(2,1)}, f32[32,1152]{1,0:T(8,128)}, f32[32,1152]{1,0:T(8,128)}) custom-call(bf16[32,1152]{1,0:T(8,128)(2,1)} %get-tuple-element.6.embed, f32[32,1152]{1,0:T(8,128)} %get-tuple-element.7.image_grad, f32[32,1152]{1,0:T(8,128)} %get-tuple-element.8.text_grad), custom_call_target="tpu_custom_call" | custom-call | tf_op jit(solution)/shard_map/hand_over/pallas_call | solution.py:541

commit v5 on v4

--- a/solution.py
+++ b/solution.py
@@ -158,18 +158,20 @@
     load_out = pltpu.make_async_copy(out_hbm, outw, load_sem.at[crop_groups + 2])
     for copy in smalls[:4]:
         copy.start()
-    for g in range(crop_groups):
+    pairs = crop_groups // 2
+    ahead = min(3, pairs)
+    for g in range(2 * ahead):
         load_crops(g).start()
     for copy in smalls[4:]:
         copy.start()
-    load_value.start()
-    load_base.start()
-    load_out.start()
-
-    column = iota((pack, pack * crop_tok), 1)
-    mine = iota((pack, pack * crop_tok), 0) == column // crop_tok
-    crop_key[...] = jnp.where(mine, column % crop_tok, 2 * crop_tok)
-    base_key = iota((pack, pack * base_tok), 0) == iota((pack, pack * base_tok), 1) // base_tok
+
+    def own_tokens(count):
+        place = iota((pack, pack * count), 1) - iota((pack, pack * count), 0) * count
+        return place, (place >= 0) & (place < count)
+
+    place, mine = own_tokens(crop_tok)
+    crop_key[...] = jnp.where(mine, place, 2 * crop_tok)
+    _, base_key = own_tokens(base_tok)
     for copy in smalls:
         copy.wait()
     len_rows[...] = jnp.broadcast_to(to_column(lengths_ref[...].astype(f32)), len_rows.shape)
@@ -192,19 +194,15 @@
             device_id_type=MESH,
         )
 
-    loop_copies = []
-
     def share_loop(n, buffer):
         for k in range(1, loops):
             peer = lax.rem(my_loop + k, loops)
-            copy = loop_copy(buffer, loop_send.at[n, k], loop_recv.at[n, k], peer, my_loop)
-            copy.start()
-            loop_copies.append(copy)
-
-    def await_loop(n, buffer):
-        for k in range(1, loops):
-            source = lax.rem(my_loop + loops - k, loops)
-            loop_copy(buffer, loop_send.at[n, k], loop_recv.at[n, k], source, source).wait_recv()
+            loop_copy(buffer, loop_send.at[n], loop_recv.at[n], peer, my_loop).start()
+
+    def all_loop(n, buffer):
+        others = pl.ds(0, loops - 1)
+        peer = lax.rem(my_loop + 1, loops)
+        return loop_copy(buffer, loop_send.at[n], loop_recv.at[n], peer, others)
 
     def pool_pair(pair, valid, groups):
         scores = [
@@ -238,6 +236,21 @@
         groups = (2 * i, 2 * i + 1)
         for g in groups:
             load_crops(g).wait()
+
+        @pl.when(i + ahead < pairs)
+        def _():
+            load_crops(2 * (i + ahead)).start()
+            load_crops(2 * (i + ahead) + 1).start()
+
+        @pl.when(i == min(1, pairs - 1))
+        def _():
+            load_value.start()
+
+        @pl.when(i == min(2, pairs - 1))
+        def _():
+            load_base.start()
+            load_out.start()
+
         pair = [tokens[pl.ds(g * pack, pack)].reshape(pack * crop_tok, width) for g in groups]
         valid = []
         for g in groups:
@@ -270,10 +283,10 @@
             h0, h1 = b0 // head_dim, (b0 + w - 1) // head_dim + 1
             rows = mixed[h0:h1, first : first + count, :].reshape((h1 - h0) * count, width)
             block = dot(rows, value[:, b0 : b0 + w]).reshape(h1 - h0, count, w)
-            head_of = (iota((1, w), 1) + b0) // head_dim
-            kept = jnp.where(head_of == h0, block[0], 0.0)
+            column = iota((1, w), 1) + b0
+            kept = block[0]
             for h in range(h0 + 1, h1):
-                kept = jnp.where(head_of == h, block[h - h0], kept)
+                kept = jnp.where(column >= h * head_dim, block[h - h0], kept)
             store(b0, w, kept)
 
     def store_crop(b0, w, block):
@@ -285,17 +298,16 @@
     def by_crop(columns_ref, first, count):
         rows = columns_ref[...].T[first // pack : (first + count) // pack, :]
         rows = jnp.broadcast_to(rows[:, None, :], (count // pack, pack, lanes))
-        keep = iota((count, lanes), 0) % pack == iota((count, lanes), 1) % pack
+        keep = (iota((count, lanes), 0) - iota((count, lanes), 1)) & (pack - 1) == 0
         return jnp.where(keep, rows.reshape(count, lanes), 0.0)
 
     meta_width = wide - width
     pieces = split(by_crop(peak_cols, 0, crops), 3) + split(by_crop(total_cols, 0, crops), 3)
     n_pieces = len(pieces)
-    k_index = iota((n_pieces * lanes, meta_width), 0)
-    gather = k_index // lanes * heads + k_index % lanes // pack == iota(
-        (n_pieces * lanes, meta_width), 1
-    )
-    meta = dot(jnp.concatenate(pieces, axis=1), gather.astype(bf16))
+    head_row = lax.shift_right_logical(iota((lanes, meta_width), 0), pack.bit_length() - 1)
+    to_head = iota((lanes, meta_width), 1) - head_row
+    gather = [(to_head == n * heads).astype(bf16) for n in range(n_pieces)]
+    meta = dot(jnp.concatenate(pieces, axis=1), jnp.concatenate(gather, axis=0))
     slot_column = to_column(slot_ref[...].astype(f32))
     meta_lane = iota((crops, meta_width), 1)
     meta = jnp.where(meta_lane == n_pieces * heads, slot_column + 1.0, meta)
@@ -307,30 +319,27 @@
     target = (owner_row * cap + rank).astype(jnp.int32)
     chosen = (iota((slots, crops), 0) == target).astype(bf16)
 
-    def crop_copy(n, sent, held, k, peer, place):
+    def crop_copy(n, sent, held, peer, source, place):
         return pltpu.make_async_remote_copy(
-            src_ref=sent.at[peer],
+            src_ref=sent.at[source],
             dst_ref=held.at[place],
-            send_sem=crop_send.at[n, k],
-            recv_sem=crop_recv.at[n, k],
+            send_sem=crop_send.at[n],
+            recv_sem=crop_recv.at[n],
             device_id=(peer, my_loop),
             device_id_type=MESH,
         )
 
-    crop_copies = []
+    def all_crops(n, sent, held):
+        others = pl.ds(0, owners - 1)
+        return crop_copy(n, sent, held, lax.rem(me + 1, owners), others, others)
 
     def share_crops(n, sent, held, rows):
         sent[...] = dot(chosen, rows).astype(bf16).reshape(sent.shape)
         for k in range(1, owners):
-            copy = crop_copy(n, sent, held, k, lax.rem(me + k, owners), me)
+            peer = lax.rem(me + k, owners)
+            copy = crop_copy(n, sent, held, peer, peer, me)
             copy.start()
-            crop_copies.append(copy)
         held[me] = sent[me]
-
-    def await_crops(n, sent, held):
-        for k in range(1, owners):
-            source = lax.rem(me + owners - k, owners)
-            crop_copy(n, sent, held, k, source, source).wait_recv()
 
     share_crops(0, meta_send, meta_recv, meta.astype(bf16))
     load_value.wait()
@@ -356,19 +365,22 @@
 
     lax.fori_loop(0, base_groups // 2, base_pair, 0)
     project(crops, images, 0, width, store_base)
-    fold = (iota((lanes, heads), 0) // pack == iota((lanes, heads), 1)).astype(bf16)
+    head_row = lax.shift_right_logical(iota((lanes, heads), 0), pack.bit_length() - 1)
+    fold = (head_row == iota((lanes, heads), 1)).astype(bf16)
 
     def folded(x):
         return sum(dot(piece, fold) for piece in split(x, 3))
 
     base_peak = folded(by_crop(peak_cols, crops, images))
     base_total = folded(by_crop(total_cols, crops, images))
-    await_crops(0, meta_send, meta_recv)
+    all_crops(0, meta_send, meta_recv).wait_recv()
 
     meta = meta_recv[...].reshape(slots, meta_width)
     m_row, m_col = iota((meta_width, meta_width), 0), iota((meta_width, meta_width), 1)
-    is_peak = (m_row < 3 * heads) & (m_row % heads == m_col)
-    is_total = (m_row >= 3 * heads) & (m_row < 6 * heads) & (m_row % heads + heads == m_col)
+    gap = m_row - m_col
+    is_peak = (m_col < heads) & ((gap == 0) | (gap == heads) | (gap == 2 * heads))
+    is_total = (gap == 2 * heads) | (gap == 3 * heads) | (gap == 4 * heads)
+    is_total = is_total & (m_col >= heads) & (m_col < 2 * heads)
     is_slot = (m_row == 6 * heads) & (m_col == 2 * heads)
     unpack = (is_peak | is_total | is_slot).astype(bf16)
     unpacked = dot(meta, unpack)
@@ -392,14 +404,15 @@
     collected = sum(dot(member_tb, piece) for piece in split(crop_total * rescale, 3))
     inverse = 1.0 / (base_total * base_rescale + collected)
     inverse_at = sum(dot(member_b, piece) for piece in split(inverse, 2))
-    widen = (iota((heads, width), 1) // head_dim == iota((heads, width), 0)).astype(bf16)
+    in_head = iota((heads, width), 1) - iota((heads, width), 0) * head_dim
+    widen = ((in_head >= 0) & (in_head < head_dim)).astype(bf16)
     crop_factor[...] = sum(dot(piece, widen) for piece in split(rescale * inverse_at, 2))
     base_factor[...] = sum(dot(piece, widen) for piece in split(base_rescale * inverse, 2))
     load_out.wait()
     gathered = [pooled_0, pooled_1, pooled_2]
     features = jnp.zeros((images, width), f32)
     for n, (c0, c1) in enumerate(chunks):
-        await_crops(n + 1, *buffers[n])
+        all_crops(n + 1, *buffers[n]).wait_recv()
         arrived = buffers[n][1][...].reshape(slots, c1 - c0).astype(f32)
         scaled = (arrived * crop_factor[:, c0:c1]).astype(bf16)
         pooled = base_sum[:, c0:c1] * base_factor[:, c0:c1] + dot(member_tb, scaled)
@@ -408,7 +421,7 @@
         features += dot(pooled.astype(bf16), outw[c0:c1, :])
     embed_ref[...] = features.astype(bf16)
     image_unit = unit_rows(features)
-    await_loop(0, text_all)
+    all_loop(0, text_all).wait_recv()
 
     scale = scale_ref[0]
     bias = bias_ref[0]
@@ -427,11 +440,13 @@
 
     features = jnp.zeros((group, width), f32)
     for n, (c0, c1) in enumerate(chunks):
-        await_loop(n + 1, gathered[n])
+        all_loop(n + 1, gathered[n]).wait_recv()
         features += dot(gathered[n][...].reshape(group, c1 - c0), outw[c0:c1, :])
     text_grad_ref[...] = gradient(unit_rows(features), text_all[my_loop, :, :width])
-    for copy in loop_copies + crop_copies:
-        copy.wait_send()
+    for n, buffer in enumerate([text_all] + gathered):
+        all_loop(n, buffer).wait_send()
+    for n, (sent, held) in enumerate([(meta_send, meta_recv)] + buffers):
+        all_crops(n, sent, held).wait_send()
 
 
 def hand_over(embed, image_grad, text_grad, embed_out, image_out, text_out):
@@ -511,10 +526,10 @@
             pltpu.VMEM((groups, (heads - heads // 2) * pack, pack * crop_tok), bf16),
             pltpu.SemaphoreType.DMA((groups + 3,)),
             pltpu.SemaphoreType.DMA((6,)),
-            pltpu.SemaphoreType.DMA((len(chunks) + 1, loops)),
-            pltpu.SemaphoreType.DMA((len(chunks) + 1, loops)),
-            pltpu.SemaphoreType.DMA((len(chunks) + 1, owners)),
-            pltpu.SemaphoreType.DMA((len(chunks) + 1, owners)),
+            pltpu.SemaphoreType.DMA((len(chunks) + 1,)),
+            pltpu.SemaphoreType.DMA((len(chunks) + 1,)),
+            pltpu.SemaphoreType.DMA((len(chunks) + 1,)),
+            pltpu.SemaphoreType.DMA((len(chunks) + 1,)),
         ],
         compiler_params=pltpu.CompilerParams(
             collective_id=0, has_side_effects=True, vmem_limit_bytes=56 * 1024 * 1024

time: 33.2 us -> 30.4 us (0.916)
  Pallas kernels: 31.1 us -> 28.3 us
    pallas_call x1, Pallas kernels: 29.3 us -> 26.5 us  [per_device(): step(crop_lengths, crop_owner.reshape(1, crops), crop_slot.reshape(1, cro...]
where the time goes in v5:
time: 30.4 us; the launch traced here: 30.2 us
  Pallas kernels  28.3 us (93%)
  between operations  1.93 us (6%)
    pallas_call x1, Pallas kernels, per_device(): step(crop_lengths, crop_owner.reshape(1, crops), crop_slot.reshape(1, cro...  26.5 us
    pallas_call x1, Pallas kernels, per_device(): pl.pallas_call(hand_over, out_shape=tuple((jax.ShapeDtypeStruct(r.shape,...  1.76 us

profile of v5, /device:TPU:0, one launch (start us, length us, event | category | flops | bytes accessed | tf_op | source)
XLA Modules:
  0.0 30.2 jit_solution(1023935110231864459)
XLA Ops:
  1.9 26.5 %contrastive_step.1 = (bf16[32,1152]{1,0:T(8,128)(2,1)}, f32[32,1152]{1,0:T(8,128)}, f32[32,1152]{1,0:T(8,128)}) custom-call(s32[1,64]{1,0:T(1,128)} %lengths_hbm.1, s32[1,64]{1,0:T(1,128)} %bitcast.5, s32[1,64]{1,0:T(1,128)} %bitcast.6, bf16[16,1152]{1,0:T(8,128)(2,1)} %bitcast.4, bf16[32,1152]{1,0:T(8,128)(2,1)} %text_hbm.1, s32[1,32]{1,0:T(1,128)} %bitcast.7, ...), custom_call_target="tpu_custom_call" | custom-call | flops 717225984 | bytes 17825792 | tf_op jit(solution)/shard_map/contrastive_step/pallas_call | solution.py:542
  28.4 1.8 %hand_over.1 = (bf16[32,1152]{1,0:T(8,128)(2,1)}, f32[32,1152]{1,0:T(8,128)}, f32[32,1152]{1,0:T(8,128)}) custom-call(bf16[32,1152]{1,0:T(8,128)(2,1)} %get-tuple-element.6.embed, f32[32,1152]{1,0:T(8,128)} %get-tuple-element.7.image_grad, f32[32,1152]{1,0:T(8,128)} %get-tuple-element.8.text_grad), custom_call_target="tpu_custom_call" | custom-call | tf_op jit(solution)/shard_map/hand_over/pallas_call | solution.py:556

commit v6 on v5

--- a/solution.py
+++ b/solution.py
@@ -105,6 +105,11 @@
     pooled_1,
     pooled_2,
     weights,
+    gather_all,
+    slot_rows,
+    chosen,
+    unpack,
+    widen,
     load_sem,
     small_sem,
     loop_send,
@@ -178,6 +183,28 @@
     peak_cols[...] = jnp.zeros_like(peak_cols)
     total_cols[...] = jnp.zeros_like(total_cols)
 
+    n_pieces, meta_width = 6, wide - width
+    head_row = lax.shift_right_logical(iota((lanes, meta_width), 0), pack.bit_length() - 1)
+    to_head = iota((lanes, meta_width), 1) - head_row
+    for n in range(n_pieces):
+        gather_all[pl.ds(n * lanes, lanes), :] = (to_head == n * heads).astype(bf16)
+    slot_rows[...] = jnp.broadcast_to(to_column(slot_ref[...].astype(f32)) + 1.0, slot_rows.shape)
+    owner_row = owner_ref[...].astype(f32)
+    owner_column = to_column(owner_row)
+    earlier = (owner_column == owner_row) & (iota((crops, crops), 0) < iota((crops, crops), 1))
+    rank = jnp.sum(jnp.where(earlier, 1.0, 0.0), axis=0, keepdims=True)
+    target = (owner_row * cap + rank).astype(jnp.int32)
+    chosen[...] = (iota((slots, crops), 0) == target).astype(bf16)
+    m_row, m_col = iota((meta_width, meta_width), 0), iota((meta_width, meta_width), 1)
+    gap = m_row - m_col
+    is_peak = (m_col < heads) & ((gap == 0) | (gap == heads) | (gap == 2 * heads))
+    is_total = (gap == 2 * heads) | (gap == 3 * heads) | (gap == 4 * heads)
+    is_total = is_total & (m_col >= heads) & (m_col < 2 * heads)
+    is_slot = (m_row == 6 * heads) & (m_col == 2 * heads)
+    unpack[...] = (is_peak | is_total | is_slot).astype(bf16)
+    in_head = iota((heads, width), 1) - iota((heads, width), 0) * head_dim
+    widen[...] = ((in_head >= 0) & (in_head < head_dim)).astype(bf16)
+
     text_unit = unit_rows(text_ref[...].astype(f32))
     labels = labels_ref[...].astype(f32)
     label_block = jnp.broadcast_to(to_column(labels), (images, wide - width)).astype(bf16)
@@ -301,23 +328,11 @@
         keep = (iota((count, lanes), 0) - iota((count, lanes), 1)) & (pack - 1) == 0
         return jnp.where(keep, rows.reshape(count, lanes), 0.0)
 
-    meta_width = wide - width
     pieces = split(by_crop(peak_cols, 0, crops), 3) + split(by_crop(total_cols, 0, crops), 3)
-    n_pieces = len(pieces)
-    head_row = lax.shift_right_logical(iota((lanes, meta_width), 0), pack.bit_length() - 1)
-    to_head = iota((lanes, meta_width), 1) - head_row
-    gather = [(to_head == n * heads).astype(bf16) for n in range(n_pieces)]
-    meta = dot(jnp.concatenate(pieces, axis=1), jnp.concatenate(gather, axis=0))
-    slot_column = to_column(slot_ref[...].astype(f32))
+    meta = dot(jnp.concatenate(pieces, axis=1), gather_all[...])
     meta_lane = iota((crops, meta_width), 1)
-    meta = jnp.where(meta_lane == n_pieces * heads, slot_column + 1.0, meta)
-
-    owner_row = owner_ref[...].astype(f32)
-    owner_column = to_column(owner_row)
-    earlier = (owner_column == owner_row) & (iota((crops, crops), 0) < iota((crops, crops), 1))
-    rank = jnp.sum(jnp.where(earlier, 1.0, 0.0), axis=0, keepdims=True)
-    target = (owner_row * cap + rank).astype(jnp.int32)
-    chosen = (iota((slots, crops), 0) == target).astype(bf16)
+    meta = jnp.where(meta_lane == n_pieces * heads, slot_rows[...], meta)
+
 
     def crop_copy(n, sent, held, peer, source, place):
         return pltpu.make_async_remote_copy(
@@ -334,7 +349,7 @@
         return crop_copy(n, sent, held, lax.rem(me + 1, owners), others, others)
 
     def share_crops(n, sent, held, rows):
-        sent[...] = dot(chosen, rows).astype(bf16).reshape(sent.shape)
+        sent[...] = dot(chosen[...], rows).astype(bf16).reshape(sent.shape)
         for k in range(1, owners):
             peer = lax.rem(me + k, owners)
             copy = crop_copy(n, sent, held, peer, peer, me)
@@ -376,18 +391,11 @@
     all_crops(0, meta_send, meta_recv).wait_recv()
 
     meta = meta_recv[...].reshape(slots, meta_width)
-    m_row, m_col = iota((meta_width, meta_width), 0), iota((meta_width, meta_width), 1)
-    gap = m_row - m_col
-    is_peak = (m_col < heads) & ((gap == 0) | (gap == heads) | (gap == 2 * heads))
-    is_total = (gap == 2 * heads) | (gap == 3 * heads) | (gap == 4 * heads)
-    is_total = is_total & (m_col >= heads) & (m_col < 2 * heads)
-    is_slot = (m_row == 6 * heads) & (m_col == 2 * heads)
-    unpack = (is_peak | is_total | is_slot).astype(bf16)
-    unpacked = dot(meta, unpack)
+    unpacked = dot(meta, unpack[...])
     crop_peak = unpacked[:, :heads]
     crop_total = unpacked[:, heads : 2 * heads]
     slot_at = unpacked[:, 2 * heads : 2 * heads + 1]
-    across = dot(unpack, meta, ((0,), (1,)))
+    across = dot(unpack[...], meta, ((0,), (1,)))
     slot_row = across[2 * heads : 2 * heads + 1, :]
     member = slot_at == iota((slots, images), 1).astype(f32) + 1.0
     member_t = slot_row == iota((images, slots), 0).astype(f32) + 1.0
@@ -404,10 +412,8 @@
     collected = sum(dot(member_tb, piece) for piece in split(crop_total * rescale, 3))
     inverse = 1.0 / (base_total * base_rescale + collected)
     inverse_at = sum(dot(member_b, piece) for piece in split(inverse, 2))
-    in_head = iota((heads, width), 1) - iota((heads, width), 0) * head_dim
-    widen = ((in_head >= 0) & (in_head < head_dim)).astype(bf16)
-    crop_factor[...] = sum(dot(piece, widen) for piece in split(rescale * inverse_at, 2))
-    base_factor[...] = sum(dot(piece, widen) for piece in split(base_rescale * inverse, 2))
+    crop_factor[...] = sum(dot(piece, widen[...]) for piece in split(rescale * inverse_at, 2))
+    base_factor[...] = sum(dot(piece, widen[...]) for piece in split(base_rescale * inverse, 2))
     load_out.wait()
     gathered = [pooled_0, pooled_1, pooled_2]
     features = jnp.zeros((images, width), f32)
@@ -449,10 +455,17 @@
         all_crops(n, sent, held).wait_send()
 
 
-def hand_over(embed, image_grad, text_grad, embed_out, image_out, text_out):
-    embed_out[...] = embed[...]
-    image_out[...] = image_grad[...]
-    text_out[...] = text_grad[...]
+def hand_over(embed, image_grad, text_grad, embed_out, image_out, text_out, sem):
+    copies = [
+        pltpu.make_async_copy(source, held, sem.at[i])
+        for i, (source, held) in enumerate(
+            [(image_grad, image_out), (text_grad, text_out), (embed, embed_out)]
+        )
+    ]
+    for copy in copies:
+        copy.start()
+    for copy in copies:
+        copy.wait()
 
 
 def per_device(
@@ -491,9 +504,9 @@
     step = pl.pallas_call(
         functools.partial(step_kernel, (owners, loops, cap)),
         out_shape=(
-            jax.ShapeDtypeStruct((images, width), bf16),
-            jax.ShapeDtypeStruct((images, width), f32),
-            jax.ShapeDtypeStruct((images, width), f32),
+            pltpu.VMEM((images, width), bf16),
+            pltpu.VMEM((images, width), f32),
+            pltpu.VMEM((images, width), f32),
         ),
         in_specs=[hbm] * 6 + [smem] * 2 + [hbm] * 4,
         out_specs=(vmem, vmem, vmem),
@@ -524,6 +537,11 @@
             pltpu.VMEM((loops, images, wide), bf16),
             *[pltpu.VMEM((loops, images, c1 - c0), bf16) for c0, c1 in chunks],
             pltpu.VMEM((groups, (heads - heads // 2) * pack, pack * crop_tok), bf16),
+            pltpu.VMEM((6 * lanes, wide - width), bf16),
+            pltpu.VMEM((crops, wide - width), f32),
+            pltpu.VMEM((owners * cap, crops), bf16),
+            pltpu.VMEM((wide - width, wide - width), bf16),
+            pltpu.VMEM((heads, width), bf16),
             pltpu.SemaphoreType.DMA((groups + 3,)),
             pltpu.SemaphoreType.DMA((6,)),
             pltpu.SemaphoreType.DMA((len(chunks) + 1,)),
@@ -557,8 +575,9 @@
         hand_over,
         out_shape=tuple(jax.ShapeDtypeStruct(r.shape, r.dtype) for r in results),
         in_specs=[vmem] * 3,
-        out_specs=(vmem, vmem, vmem),
-        compiler_params=pltpu.CompilerParams(vmem_limit_bytes=56 * 1024 * 1024),
+        out_specs=(hbm, hbm, hbm),
+        scratch_shapes=[pltpu.SemaphoreType.DMA((3,))],
+        compiler_params=pltpu.CompilerParams(vmem_limit_bytes=4 * 1024 * 1024),
         name="hand_over",
     )(*results)
 

time: 30.4 us -> 28.7 us (0.944)
  Pallas kernels: 28.3 us -> 26.6 us
    pallas_call x1, Pallas kernels: 1.76 us -> 0.76 us  [per_device(): pl.pallas_call(hand_over, out_shape=tuple((jax.ShapeDtypeStruct(r.shape,...]
    pallas_call x1, Pallas kernels: 26.5 us -> 25.8 us  [per_device(): step(crop_lengths, crop_owner.reshape(1, crops), crop_slot.reshape(1, cro...]
where the time goes in v6:
time: 28.7 us; the launch traced here: 28.5 us
  Pallas kernels  26.6 us (93%)
  between operations  1.93 us (7%)
    pallas_call x1, Pallas kernels, per_device(): step(crop_lengths, crop_owner.reshape(1, crops), crop_slot.reshape(1, cro...  25.8 us
    pallas_call x1, Pallas kernels, per_device(): pl.pallas_call(hand_over, out_shape=tuple((jax.ShapeDtypeStruct(r.shape,...  0.76 us

profile of v6, /device:TPU:0, one launch (start us, length us, event | category | flops | bytes accessed | tf_op | source)
XLA Modules:
  0.0 28.5 jit_solution(16780579218489594968)
XLA Ops:
  1.9 25.8 %contrastive_step.1 = (bf16[32,1152]{1,0:T(8,128)(2,1)S(1)}, f32[32,1152]{1,0:T(8,128)S(1)}, f32[32,1152]{1,0:T(8,128)S(1)}) custom-call(s32[1,64]{1,0:T(1,128)} %lengths_hbm.1, s32[1,64]{1,0:T(1,128)} %bitcast.5, s32[1,64]{1,0:T(1,128)} %bitcast.6, bf16[16,1152]{1,0:T(8,128)(2,1)} %bitcast.4, bf16[32,1152]{1,0:T(8,128)(2,1)} %text_hbm.1, s32[1,32]{1,0:T(1,128)} %bitcast.7, ...), custom_call_target="tpu_custom_call" | custom-call | flops 717225984 | bytes 17825792 | tf_op jit(solution)/shard_map/contrastive_step/pallas_call | solution.py:560
  27.8 0.8 %hand_over.1 = (bf16[32,1152]{1,0:T(8,128)(2,1)}, f32[32,1152]{1,0:T(8,128)}, f32[32,1152]{1,0:T(8,128)}) custom-call(bf16[32,1152]{1,0:T(8,128)(2,1)S(1)} %get-tuple-element.6.embed, f32[32,1152]{1,0:T(8,128)S(1)} %get-tuple-element.7.image_grad, f32[32,1152]{1,0:T(8,128)S(1)} %get-tuple-element.8.text_grad), custom_call_target="tpu_custom_call" | custom-call | tf_op jit(solution)/shard_map/hand_over/pallas_call | solution.py:574

commit v7 on v6

--- a/solution.py
+++ b/solution.py
@@ -144,6 +144,19 @@
         )
     ]
 
+    def load_crops(g):
+        part = pl.ds(g * pack, pack)
+        return pltpu.make_async_copy(tokens_hbm.at[part], tokens.at[part], load_sem.at[g])
+
+    load_value = pltpu.make_async_copy(value_hbm, value, load_sem.at[crop_groups])
+    load_base = pltpu.make_async_copy(base_hbm, base, load_sem.at[crop_groups + 1])
+    load_out = pltpu.make_async_copy(out_hbm, outw, load_sem.at[crop_groups + 2])
+    for copy in smalls:
+        copy.start()
+    pairs = crop_groups // 2
+    ahead = min(3, pairs)
+    for g in range(2 * ahead):
+        load_crops(g).start()
     barrier = pltpu.get_barrier_semaphore()
     for k in range(1, owners):
         pl.semaphore_signal(
@@ -153,22 +166,6 @@
         pl.semaphore_signal(
             barrier, inc=1, device_id=(me, lax.rem(my_loop + k, loops)), device_id_type=MESH
         )
-
-    def load_crops(g):
-        part = pl.ds(g * pack, pack)
-        return pltpu.make_async_copy(tokens_hbm.at[part], tokens.at[part], load_sem.at[g])
-
-    load_value = pltpu.make_async_copy(value_hbm, value, load_sem.at[crop_groups])
-    load_base = pltpu.make_async_copy(base_hbm, base, load_sem.at[crop_groups + 1])
-    load_out = pltpu.make_async_copy(out_hbm, outw, load_sem.at[crop_groups + 2])
-    for copy in smalls[:4]:
-        copy.start()
-    pairs = crop_groups // 2
-    ahead = min(3, pairs)
-    for g in range(2 * ahead):
-        load_crops(g).start()
-    for copy in smalls[4:]:
-        copy.start()
 
     def own_tokens(count):
         place = iota((pack, pack * count), 1) - iota((pack, pack * count), 0) * count

time: 28.7 us -> 28.2 us (0.983)
  Pallas kernels: 26.6 us -> 26.2 us
    pallas_call x1, Pallas kernels: 25.8 us -> 25.4 us  [per_device(): step(crop_lengths, crop_owner.reshape(1, crops), crop_slot.reshape(1, cro...]
where the time goes in v7:
time: 28.2 us; the launch traced here: 28.1 us
  Pallas kernels  26.2 us (93%)
  between operations  1.93 us (7%)
    pallas_call x1, Pallas kernels, per_device(): step(crop_lengths, crop_owner.reshape(1, crops), crop_slot.reshape(1, cro...  25.4 us
    pallas_call x1, Pallas kernels, per_device(): pl.pallas_call(hand_over, out_shape=tuple((jax.ShapeDtypeStruct(r.shape,...  0.76 us

profile of v7, /device:TPU:0, one launch (start us, length us, event | category | flops | bytes accessed | tf_op | source)
XLA Modules:
  0.0 28.1 jit_solution(9355417919510074179)
XLA Ops:
  1.9 25.4 %contrastive_step.1 = (bf16[32,1152]{1,0:T(8,128)(2,1)S(1)}, f32[32,1152]{1,0:T(8,128)S(1)}, f32[32,1152]{1,0:T(8,128)S(1)}) custom-call(s32[1,64]{1,0:T(1,128)} %lengths_hbm.1, s32[1,64]{1,0:T(1,128)} %bitcast.5, s32[1,64]{1,0:T(1,128)} %bitcast.6, bf16[16,1152]{1,0:T(8,128)(2,1)} %bitcast.4, bf16[32,1152]{1,0:T(8,128)(2,1)} %text_hbm.1, s32[1,32]{1,0:T(1,128)} %bitcast.7, ...), custom_call_target="tpu_custom_call" | custom-call | flops 717225984 | bytes 17825792 | tf_op jit(solution)/shard_map/contrastive_step/pallas_call | solution.py:557
  27.3 0.8 %hand_over.1 = (bf16[32,1152]{1,0:T(8,128)(2,1)}, f32[32,1152]{1,0:T(8,128)}, f32[32,1152]{1,0:T(8,128)}) custom-call(bf16[32,1152]{1,0:T(8,128)(2,1)S(1)} %get-tuple-element.6.embed, f32[32,1152]{1,0:T(8,128)S(1)} %get-tuple-element.7.image_grad, f32[32,1152]{1,0:T(8,128)S(1)} %get-tuple-element.8.text_grad), custom_call_target="tpu_custom_call" | custom-call | tf_op jit(solution)/shard_map/hand_over/pallas_call | solution.py:571
